TPU v7x, 256 devices: a whole 4x4x8 slice. The times are simulated.
256 devices in a mesh: lat: 16 (over x_hi, z), lon: 16 (over x_lo, y, core).
Axes of the slice: x: 4 (x_hi: 2, x_lo: 2; x = x_hi * 2 + x_lo), y: 4, z: 8, core: 2. Of those that a mesh axis runs over, the one named last changes fastest.
Arguments:
- fields: bfloat16 [2, 192, 288, 384], P(None, 'lat', 'lon'), may hold values from -6 to 6
- cotangent: bfloat16 [2, 192, 288, 384], P(None, 'lat', 'lon'), may hold values from -6 to 6
- norm_gain: float32 [384], replicated, may hold values from 0.5 to 1.5
- w_query: bfloat16 [384, 384], P('lat', 'lon'), may hold values from -0.3125 to 0.3125
- w_key: bfloat16 [384, 384], P('lat', 'lon'), may hold values from -0.3125 to 0.3125
- w_value: bfloat16 [384, 384], P('lat', 'lon'), may hold values from -0.3125 to 0.3125
- w_out: bfloat16 [384, 384], P('lat', 'lon'), may hold values from -0.3125 to 0.3125
- rel_table: float32 [16, 12, 6336], P('lat'), may hold values from -4 to 304
Outputs:
- grad_fields: bfloat16 [2, 192, 288, 384], P(None, 'lat', 'lon')
- grad_query: float32 [384, 384], P('lat', 'lon')
- grad_key: float32 [384, 384], P('lat', 'lon')
- grad_value: float32 [384, 384], P('lat', 'lon')
- grad_out: float32 [384, 384], P('lat', 'lon')
- grad_table: float32 [16, 12, 6336], P('lat', None, 'lon')
- grad_gain: float32 [384], replicated
All inputs are finite; a program needn't handle non-finite values.
Results may differ from a plain program's by a relative error of at most 0.03.
Values may be sent and summed in bfloat16 or wider, within the bound.
No kernel may reach another device: no remote copies, remote signals or barrier semaphores. Data moves between devices by JAX's collectives and lax.ppermute only.
A program may use at most 128 MiB of HBM per device.

v0:
```python
import functools
import math

import jax
import jax.numpy as jnp
import numpy as np
from jax import lax
from jax.experimental import pallas as pl
from jax.experimental.pallas import tpu as pltpu
from jax.sharding import PartitionSpec as P

EPSILON = 1e-05
MASKED = -1000000000.0
LOG2E = math.log2(math.e)
UNROLL = 6
BLOCK_MB = 28
SMALL_MB = 16
F32 = jnp.float32
BF16 = jnp.bfloat16
NN = (((1,), (0,)), ((), ()))
NT = (((1,), (1,)), ((), ()))
TN = (((0,), (0,)), ((), ()))


def mm(a, b, dims):
    return lax.dot_general(a, b, dims, preferred_element_type=F32)


def offset_order(rels, levels, lat_rows, group):
    lanes = rels * levels * lat_rows
    order = np.zeros((levels * group, lanes + -lanes % 128), np.float32)
    for level in range(levels):
        for lat in range(lat_rows):
            for rel in range(rels):
                order[level * group + lat * rels + rel, ((rels - 1 - rel) * levels + level) * lat_rows + lat] = 1.0
    return order


def bias_kernel(last_ref, table_ref, order_ref, out_ref, table_s, strips_s, bias_s, *, levels, lat_rows, rels, windows):
    heads = table_ref.shape[0]
    slots = table_s.shape[1]
    cell = levels * lat_rows
    width = lat_rows * rels
    group = table_s.shape[2] // levels
    tiles = strips_s.shape[0]
    lanes = tiles * 128
    lon_width = (rels + 1) // 2
    tokens = lon_width * cell
    table_s[...] = jnp.zeros_like(table_s)
    table = table_ref[...]
    for z in range(levels):
        for w in range(levels):
            for a in range(lat_rows):
                at = ((z * levels + w) * lat_rows + a) * width
                table_s[z * lat_rows + a, 0:heads, w * group:w * group + width] = table[:, at:at + width]
    full = table_s[...].reshape(cell * slots, levels * group)
    order = order_ref[...]
    high = full.astype(BF16)
    rest = full - high.astype(F32)
    mid = rest.astype(BF16)
    low = (rest - mid.astype(F32)).astype(BF16)
    strips = mm(high, order, NN) + mm(mid, order, NN) + mm(low, order, NN)
    row = lax.broadcasted_iota(jnp.int32, (cell * slots, 1), 0) // slots
    lane = lax.broadcasted_iota(jnp.int32, (1, lanes), 1)
    row_north = (row % lat_rows < lat_rows // 2).astype(F32)
    lane_north = (lane % lat_rows < lat_rows // 2).astype(F32)
    crossing = (row_north != lane_north) & (last_ref[0] != 0)
    strips = jnp.where(crossing, MASKED, strips) * LOG2E
    for g in range(tiles):
        strips_s[g] = strips[:, g * 128:(g + 1) * 128]

    def head(h, carry):
        strip = jnp.concatenate([strips_s[g, pl.ds(h, cell, stride=slots), :] for g in range(tiles)], axis=1)
        for p in range(lon_width):
            off = (lon_width - 1 - p) * cell
            rolled = pltpu.roll(strip, lanes - off, 1) if off else strip
            bias_s[p * cell:(p + 1) * cell, :] = rolled[:, :tokens]
        bias = bias_s[...].T
        out_ref[h] = jnp.concatenate([bias] * windows, axis=1)
        return carry

    lax.fori_loop(0, heads, head, 0)


def make_bias(last, table, order, levels, lat_rows, rels, slots, windows):
    heads = table.shape[0]
    cell = levels * lat_rows
    tokens = (rels + 1) // 2 * cell
    tiles = order.shape[1] // 128
    vmem = pl.BlockSpec(memory_space=pltpu.VMEM)
    return pl.pallas_call(
        functools.partial(bias_kernel, levels=levels, lat_rows=lat_rows, rels=rels, windows=windows),
        out_shape=jax.ShapeDtypeStruct((heads, tokens, windows * tokens), F32),
        in_specs=[pl.BlockSpec(memory_space=pltpu.SMEM), vmem, vmem],
        out_specs=vmem,
        scratch_shapes=[
            pltpu.VMEM((cell, slots, order.shape[0]), F32),
            pltpu.VMEM((tiles, cell * slots, 128), F32),
            pltpu.VMEM((tokens, tokens), F32),
        ],
        compiler_params=pltpu.CompilerParams(vmem_limit_bytes=SMALL_MB * 2**20),
        name="make_bias",
    )(last, table, order)


def turn_kernel(x_ref, out_ref):
    blocks, rows, lanes = x_ref.shape
    turned = x_ref[...].astype(F32).reshape(blocks * rows, lanes).T.astype(BF16)
    for i in range(out_ref.shape[0]):
        out_ref[i] = turned


def turn(x, copies):
    blocks, rows, lanes = x.shape
    vmem = pl.BlockSpec(memory_space=pltpu.VMEM)
    return pl.pallas_call(
        turn_kernel,
        out_shape=jax.ShapeDtypeStruct((copies, lanes, blocks * rows), BF16),
        in_specs=[vmem],
        out_specs=vmem,
        compiler_params=pltpu.CompilerParams(vmem_limit_bytes=SMALL_MB * 2**20),
        name="turn_weights",
    )(x)


def load_weights(w_s, w_same_ref, w_other_ref, parity):
    pairs, packed, _ = w_same_ref.shape
    part = packed // 4
    for ref, side in ((w_same_ref, parity), (w_other_ref, 1 - parity)):
        for i in range(pairs):
            block = ref[i].astype(F32)
            start = pl.multiple_of((2 * i + side) * part, part)
            for k in range(w_s.shape[0]):
                w_s[k, pl.ds(start, part), :] = block[k * part:(k + 1) * part]


def normalise(x_ref):
    xf = x_ref[...].astype(F32)
    mean = jnp.mean(xf, axis=1, keepdims=True)
    centred = xf - mean
    var = jnp.mean(centred * centred, axis=1, keepdims=True)
    inv = 1.0 / jnp.sqrt(var + EPSILON)
    return centred * inv, inv


def block_kernel(
    me_ref, x_ref, c_ref, gain_ref, w_same_ref, w_other_ref, bias_ref, order_ref,
    same_ref, other_ref, dq_s, dk_s, dv_s,
    w_s, gw_s, normed_s, q_s, d_s, k_s, v_s, ctx_s, dsum_s, fold_s, pick_s,
    *, heads, windows, levels, lat_rows, rels,
):
    feat = x_ref.shape[1]
    dim = feat // heads
    lon_width = (rels + 1) // 2
    cell = levels * lat_rows
    tokens = lon_width * cell
    scale = 1.0 / math.sqrt(dim)
    tiles = fold_s.shape[0]
    lanes = tiles * 128
    slots = fold_s.shape[1] // cell
    pairs, packed, _ = w_same_ref.shape
    part = packed // 4
    parity = me_ref[0] % 2

    load_weights(w_s, w_same_ref, w_other_ref, parity)
    std, _ = normalise(x_ref)
    normed_s[...] = (std * gain_ref[...]).astype(BF16)
    window = lax.broadcasted_iota(jnp.int32, (dim, windows * tokens), 1) // tokens

    def apart(x):
        x = x.astype(BF16).reshape(heads, dim, windows * tokens)
        return [jnp.where((window == w)[None], x, jnp.zeros_like(x)) for w in range(windows)]

    w_qry = w_s[0].astype(BF16)
    w_key = w_s[1].astype(BF16)
    w_val = w_s[2].astype(BF16)
    w_out = w_s[3].T.astype(BF16)
    for dst, x in ((q_s, mm(w_qry, normed_s[...], NT)), (d_s, mm(w_out, c_ref[...], NT))):
        for w, block in enumerate(apart(x)):
            dst[:, w * dim:(w + 1) * dim, :] = block
    for w in range(windows):
        nw = normed_s[w * tokens:(w + 1) * tokens]
        k_s[:, w * dim:(w + 1) * dim, :] = mm(w_key, nw, NT).astype(BF16).reshape(heads, dim, tokens)
        v_s[:, w * dim:(w + 1) * dim, :] = mm(w_val, nw, NT).astype(BF16).reshape(heads, dim, tokens)
    query = lax.broadcasted_iota(jnp.int32, (tokens, tokens * windows), 1) % tokens
    pick_s[...] = (query == lax.broadcasted_iota(jnp.int32, query.shape, 0)).astype(F32).astype(BF16)
    dsum_s[...] = jnp.zeros_like(dsum_s)
    fold_s[...] = jnp.zeros_like(fold_s)

    def own(x):
        out = x[:dim]
        for w in range(1, windows):
            out = jnp.where(window == w, x[w * dim:(w + 1) * dim], out)
        return out

    def head(h, carry):
        qh, dh, kh, vh = q_s[h], d_s[h], k_s[h], v_s[h]
        score = mm(kh, qh, TN) * (scale * LOG2E) + bias_ref[h]
        d_prob = mm(vh, dh, TN)
        expo = jnp.exp2(score - jnp.max(score, axis=0, keepdims=True))
        prob = expo * (1.0 / jnp.sum(expo, axis=0, keepdims=True))
        low = prob.astype(BF16)
        ctx = own(mm(vh, low, NN))
        ctx_s[h] = ctx.astype(BF16)
        dv_s[h] = mm(dh, low, NT).astype(BF16)
        d_ctx = dh[:dim].astype(F32)
        for w in range(1, windows):
            d_ctx = d_ctx + dh[w * dim:(w + 1) * dim].astype(F32)
        inner = jnp.sum(ctx * d_ctx, axis=0, keepdims=True)
        d_low = (prob * (d_prob - inner)).astype(BF16)
        dq_s[h] = (own(mm(kh, d_low, NN)) * scale).astype(BF16)
        both = mm(jnp.concatenate([qh, pick_s[...]], axis=0), d_low, NT)
        dk_s[h] = (both[:windows * dim] * scale).astype(BF16)
        dsum_s[:, :tokens] = both[windows * dim:]
        folded = jnp.zeros((cell, lanes), F32)
        for p in range(lon_width):
            off = (lon_width - 1 - p) * cell
            piece = dsum_s[p * cell:(p + 1) * cell, :]
            folded = folded + (pltpu.roll(piece, off, 1) if off else piece)
        for g in range(tiles):
            fold_s[g, pl.ds(h, cell, stride=slots), :] = folded[:, g * 128:(g + 1) * 128]
        return carry

    if UNROLL:
        lax.fori_loop(0, heads, head, 0, unroll=UNROLL)

    def by_window(ref, w):
        return ref[:, w * dim:(w + 1) * dim, :].reshape(feat, tokens)

    gw_s[0] = mm(dq_s[...].reshape(feat, windows * tokens), normed_s[...], NN)
    gw_s[3] = mm(ctx_s[...].reshape(feat, windows * tokens), c_ref[...], NN).T
    for i, ref in ((1, dk_s), (2, dv_s)):
        total = jnp.zeros((feat, feat), F32)
        for w in range(windows):
            total = total + mm(by_window(ref, w), normed_s[w * tokens:(w + 1) * tokens], NN)
        gw_s[i] = total
    g_gain = jnp.zeros((1, feat), F32)
    for i in range(3):
        g_gain = g_gain + jnp.sum(gw_s[i] * w_s[i], axis=0, keepdims=True)
    g_gain = g_gain / gain_ref[...]

    fold = jnp.concatenate([fold_s[g] for g in range(tiles)], axis=1).astype(BF16)
    back = mm(fold, order_ref[...], NT)
    width = lat_rows * rels
    half = back.shape[1] // levels
    per = 2 * pairs // (levels * levels)
    run = lat_rows // per
    wide = -(-run * width // 128) * 128
    back = back.reshape(levels * per, run, slots, levels * half)
    full = []
    for w in range(levels):
        line = jnp.zeros((levels * per * slots, wide), F32)
        for k in range(run):
            piece = back[:, k, :, w * half:(w + 1) * half].reshape(levels * per * slots, half)
            piece = jnp.concatenate([piece, jnp.zeros((levels * per * slots, wide - half), F32)], axis=1)
            line = line + (pltpu.roll(piece, k * width, 1) if k else piece)
        full.append(line)

    lane = lax.broadcasted_iota(jnp.int32, (8, feat), 1) % 128
    row = lax.broadcasted_iota(jnp.int32, (8, feat), 0)
    gains = jnp.zeros((8, feat), F32)
    for i in range(4):
        turned = jnp.concatenate(
            [pltpu.roll(g_gain[:, g * 128:(g + 1) * 128], (160 - 32 * i) % 128, 1) for g in range(feat // 128)], axis=1
        )
        gains = jnp.where((row == 4 + i) & (lane >= 32) & (lane < 64), turned, gains)

    for ref, side in ((same_ref, parity), (other_ref, 1 - parity)):
        for i in range(pairs):
            start = pl.multiple_of((2 * i + side) * part, part)
            block = jnp.concatenate([gw_s[k, pl.ds(start, part), :] for k in range(4)], axis=0)
            ref[i, 0:packed, :] = block.astype(BF16)
    for j in range(2 * pairs):
        z, w, a = j // (levels * per), j // per % levels, j % per
        at = (z * per + a) * slots
        line = full[w][at:at + slots]
        tail = line[:, feat:]
        moved = jnp.concatenate([pltpu.roll(tail[:8], 4, 0), tail[:8], pltpu.roll(tail[8:], 4, 0)], axis=1)
        moved = jnp.where(lane < 32, moved, gains)
        lines = jnp.concatenate([line[:8, :feat], jnp.where(row >= 4, moved, line[8:, :feat])], axis=0).astype(BF16)

        @pl.when(parity == j % 2)
        def _():
            same_ref[j // 2, packed:, :] = lines

        @pl.when(parity != j % 2)
        def _():
            other_ref[j // 2, packed:, :] = lines


def run_block(me, x, c, gain, w_same, w_other, bias, order, heads, windows, levels, lat_rows, rels):
    rows, feat = x.shape
    tokens = rows // windows
    dim = feat // heads
    cell = levels * lat_rows
    tiles = order.shape[1] // 128
    slots = heads + -heads % 16
    pairs, packed, _ = w_same.shape
    vmem = pl.BlockSpec(memory_space=pltpu.VMEM)
    sent = jax.ShapeDtypeStruct((pairs, packed + slots, feat), BF16)
    aligned = jax.ShapeDtypeStruct((heads, windows * dim, tokens), BF16)
    return pl.pallas_call(
        functools.partial(block_kernel, heads=heads, windows=windows, levels=levels, lat_rows=lat_rows, rels=rels),
        out_shape=(sent, sent, jax.ShapeDtypeStruct((heads, dim, rows), BF16), aligned, aligned),
        in_specs=[pl.BlockSpec(memory_space=pltpu.SMEM)] + [vmem] * 7,
        out_specs=[vmem] * 5,
        scratch_shapes=[
            pltpu.VMEM((4, feat, feat), F32),
            pltpu.VMEM((4, feat, feat), F32),
            pltpu.VMEM((rows, feat), BF16),
            pltpu.VMEM((heads, windows * dim, rows), BF16),
            pltpu.VMEM((heads, windows * dim, rows), BF16),
            pltpu.VMEM((heads, windows * dim, tokens), BF16),
            pltpu.VMEM((heads, windows * dim, tokens), BF16),
            pltpu.VMEM((heads, dim, rows), BF16),
            pltpu.VMEM((tokens, tiles * 128), F32),
            pltpu.VMEM((tiles, cell * slots, 128), F32),
            pltpu.VMEM((tokens, rows), BF16),
        ],
        compiler_params=pltpu.CompilerParams(vmem_limit_bytes=BLOCK_MB * 2**20),
        name="window_block",
    )(me, x, c, gain, w_same, w_other, bias, order)


def input_kernel(me_ref, x_ref, gain_ref, w_same_ref, w_other_ref, dq_ref, dk_ref, dv_ref, din_ref, w_s):
    heads, stacked, tokens = dk_ref.shape
    rows, feat = x_ref.shape
    windows = rows // tokens
    dim = stacked // windows
    load_weights(w_s, w_same_ref, w_other_ref, me_ref[0] % 2)
    std, inv = normalise(x_ref)
    gain = gain_ref[...]
    w_qry, w_key, w_val = (w_s[i].astype(BF16) for i in range(3))
    from_q = mm(dq_ref[...].reshape(feat, rows), w_qry, TN)
    for w in range(windows):
        at = slice(w * tokens, (w + 1) * tokens)
        d_normed = from_q[at]
        for ref, weight in ((dk_ref, w_key), (dv_ref, w_val)):
            d_normed = d_normed + mm(ref[:, w * dim:(w + 1) * dim, :].reshape(feat, tokens), weight, TN)
        g = d_normed * gain
        d_in = inv[at] * (
            g - jnp.mean(g, axis=1, keepdims=True) - std[at] * jnp.mean(g * std[at], axis=1, keepdims=True)
        )
        din_ref[at] = d_in.astype(BF16)


def input_gradient(me, x, gain, w_same, w_other, dq, dk, dv):
    feat = x.shape[1]
    vmem = pl.BlockSpec(memory_space=pltpu.VMEM)
    return pl.pallas_call(
        input_kernel,
        out_shape=jax.ShapeDtypeStruct(x.shape, BF16),
        in_specs=[pl.BlockSpec(memory_space=pltpu.SMEM)] + [vmem] * 7,
        out_specs=vmem,
        scratch_shapes=[pltpu.VMEM((3, feat, feat), F32)],
        compiler_params=pltpu.CompilerParams(vmem_limit_bytes=SMALL_MB * 2**20),
        name="input_gradient",
    )(me, x, gain, w_same, w_other, dq, dk, dv)


def sum_kernel(x_ref, out_ref, table_ref, *, packed):
    pieces, rows, feat = x_ref.shape
    total = x_ref[0].astype(F32)
    for i in range(1, pieces):
        total = total + x_ref[i].astype(F32)
    turned = total[:packed].T
    blocks = out_ref.shape[0]
    part = feat // blocks
    lane = lax.broadcasted_iota(jnp.int32, (1, feat), 1) % 128
    gain = jnp.zeros((1, feat), F32)
    for i in range(4):
        line = total[rows - 4 + i:rows - 3 + i]
        moved = jnp.concatenate(
            [pltpu.roll(line[:, g * 128:(g + 1) * 128], (32 * i - 32) % 128, 1) for g in range(feat // 128)], axis=1
        )
        gain = jnp.where((lane >= 32 * i) & (lane < 32 * i + 32), moved, gain)
    high = gain.astype(BF16).astype(F32)
    gains = jnp.concatenate(
        [src[:, k * packed:(k + 1) * packed] for src in (high, gain - high) for k in range(feat // packed)], axis=0
    )
    for i in range(blocks):
        out_ref[i] = jnp.concatenate([turned[i * part:(i + 1) * part], gains], axis=0).astype(BF16)
    table_ref[...] = total[packed:]


def sum_and_turn(x, blocks, packed):
    pieces, rows, feat = x.shape
    vmem = pl.BlockSpec(memory_space=pltpu.VMEM)
    return pl.pallas_call(
        functools.partial(sum_kernel, packed=packed),
        out_shape=(
            jax.ShapeDtypeStruct((blocks, feat // blocks + 2 * (feat // packed), packed), BF16),
            jax.ShapeDtypeStruct((rows - packed, feat), F32),
        ),
        in_specs=[vmem],
        out_specs=[vmem, vmem],
        compiler_params=pltpu.CompilerParams(vmem_limit_bytes=SMALL_MB * 2**20),
        name="sum_and_turn",
    )(x)


def last_kernel(x_ref, query_ref, key_ref, value_ref, out_ref, gain_ref):
    total = x_ref[0].astype(F32)
    for i in range(1, x_ref.shape[0]):
        total = total + x_ref[i].astype(F32)
    part = query_ref.shape[0]
    for i, ref in enumerate((query_ref, key_ref, value_ref, out_ref)):
        ref[...] = total[:part, i * part:(i + 1) * part]
    count = (total.shape[0] - part) // 2
    gain = total[part:part + count] + total[part + count:]
    gain_ref[...] = jnp.concatenate([gain[k:k + 1] for k in range(count)], axis=1).reshape(gain_ref.shape)


def last_sum(x, part, feat):
    vmem = pl.BlockSpec(memory_space=pltpu.VMEM)
    block = jax.ShapeDtypeStruct((part, part), F32)
    return pl.pallas_call(
        last_kernel,
        out_shape=(block, block, block, block, jax.ShapeDtypeStruct((feat,), F32)),
        in_specs=[vmem],
        out_specs=[vmem] * 5,
        compiler_params=pltpu.CompilerParams(vmem_limit_bytes=SMALL_MB * 2**20),
        name="last_sum",
    )(x)


def swap(x, axis, bit):
    n = lax.axis_size(axis)
    return lax.ppermute(x, axis, [(i, i ^ bit) for i in range(n)])


def shift(x, lat_by, lon_by):
    lats, lons = lax.axis_size("lat"), lax.axis_size("lon")
    if lon_by == 0:
        return lax.ppermute(x, "lat", [(i, (i + lat_by) % lats) for i in range(lats)])
    if lat_by == 0:
        return lax.ppermute(x, "lon", [(i, (i + lon_by) % lons) for i in range(lons)])
    pairs = [
        (a * lons + b, (a + lat_by) % lats * lons + (b + lon_by) % lons)
        for a in range(lats)
        for b in range(lons)
    ]
    return lax.ppermute(x, ("lat", "lon"), pairs)


def spread_over_lat(x):
    return lax.all_to_all(x, "lat", 0, 0)


def spread_over_lon(x):
    n = lax.axis_size("lon")
    groups = [list(range(c, n, 2)) for c in range(2)]
    return lax.all_to_all(x, "lon", 0, 0, axis_index_groups=groups)


def local(fields, cotangent, norm_gain, w_query, w_key, w_value, w_out, rel_table):
    levels, lat_rows, lon_cols, feat = fields.shape
    heads = rel_table.shape[1]
    rels = rel_table.shape[2] // (levels * levels * lat_rows * lat_rows)
    lon_width = (rels + 1) // 2
    half_rows = lat_rows // 2
    half_cols = lon_width // 2
    windows = lon_cols // lon_width
    lats = lax.axis_size("lat")
    lons = lax.axis_size("lon")
    me_lat = lax.axis_index("lat")
    me_lon = lax.axis_index("lon")
    part = w_query.shape[0]

    both = jnp.stack([fields, cotangent]).transpose(3, 0, 1, 2, 4)

    mine = jnp.concatenate([w_query, w_key, w_value, w_out], axis=1)
    rows_all = spread_over_lat(jnp.broadcast_to(mine[None], (lats,) + mine.shape))
    turned = turn(rows_all, lons // 2)
    pieces = (
        both[half_cols:, :, :, half_rows:],
        both[half_cols:, :, :, :half_rows],
        both[:half_cols, :, :, half_rows:],
        both[:half_cols, :, :, :half_rows],
    )
    turned, pieces = lax.optimization_barrier((turned, pieces))
    w_same = spread_over_lon(turned)
    own = pieces[0]
    south = shift(pieces[1], -1, 0)
    east = shift(pieces[2], 0, -1)
    corner = shift(pieces[3], -1, -1)
    own, south, east, corner, table = lax.optimization_barrier((own, south, east, corner, rel_table[0]))
    moved = jnp.concatenate(
        [jnp.concatenate([own, south], axis=3), jnp.concatenate([east, corner], axis=3)], axis=0
    )
    shifted = moved[:, 0].reshape(-1, feat)
    cot_shift = moved[:, 1].reshape(-1, feat)

    order = jnp.asarray(offset_order(rels, levels, lat_rows, 256), BF16)
    last = (me_lat == lats - 1).astype(jnp.int32).reshape(1)
    slots = heads + -heads % 16
    bias = make_bias(last, table, order, levels, lat_rows, rels, slots, windows)
    w_same, bias = lax.optimization_barrier((w_same, bias))
    w_other = swap(w_same, "lon", 1)

    me = me_lon.reshape(1)
    gain = norm_gain[None]
    g_same, g_other, dq, dk, dv = run_block(
        me, shifted, cot_shift, gain, w_same, w_other, bias, order, heads, windows, levels, lat_rows, rels
    )

    paired = (g_same.astype(F32) + swap(g_other, "lon", 1).astype(F32)).astype(BF16)
    paired, dq, dk, dv = lax.optimization_barrier((paired, dq, dk, dv))
    arrived = spread_over_lon(paired)
    message, lines = sum_and_turn(arrived, lats, 4 * part)
    grad_query, grad_key, grad_value, grad_out, grad_gain = last_sum(spread_over_lat(message), part, feat)
    d_input = input_gradient(me, shifted, gain, w_same, w_other, dq, dk, dv)

    d_in = d_input.reshape(lon_cols, levels, lat_rows, feat)
    stay = lon_cols - half_cols
    west = shift(d_in[stay:, :, :half_rows], 0, 1)
    north = shift(d_in[:stay, :, half_rows:], 1, 0)
    corner = shift(d_in[stay:, :, half_rows:], 1, 1)
    west, north, corner, d_in, lines, _ = lax.optimization_barrier((west, north, corner, d_in, lines, message))
    over = rel_table.shape[2] // lons - feat
    groups = feat // 128
    tail = lines[heads:].reshape(slots - heads, groups, 128)[:, :, :over].transpose(1, 0, 2)
    grad_table = jnp.concatenate([lines[:heads], tail.reshape(heads, over)], axis=1)[None]
    back = jnp.concatenate(
        [jnp.concatenate([corner, west], axis=2), jnp.concatenate([north, d_in[:stay, :, :half_rows]], axis=2)],
        axis=0,
    ).transpose(1, 2, 0, 3)
    grad_fields = (cotangent.astype(F32) + back.astype(F32)).astype(BF16)
    return (grad_fields, grad_query, grad_key, grad_value, grad_out, grad_table, grad_gain)


def solution(mesh):
    return jax.shard_map(
        local,
        mesh=mesh,
        in_specs=(
            P(None, "lat", "lon", None),
            P(None, "lat", "lon", None),
            P(),
            P("lat", "lon"),
            P("lat", "lon"),
            P("lat", "lon"),
            P("lat", "lon"),
            P("lat", None, None),
        ),
        out_specs=(
            P(None, "lat", "lon", None),
            P("lat", "lon"),
            P("lat", "lon"),
            P("lat", "lon"),
            P("lat", "lon"),
            P("lat", None, "lon"),
            P(),
        ),
        check_vma=False,
    )
```

profile of v0, /device:TPU:8, one launch (start us, length us, event | category | flops | bytes accessed | tf_op | source)
XLA Modules:
  0.0 108.2 jit_solution(13694359791888245629)
XLA Ops:
  2.1 11.0 %all-to-all-start = ((bf16[16,24,96]{2,1,0:T(8,128)(2,1)}), bf16[16,24,96]{2,1,0:T(8,128)(2,1)S(1)}, u32[]{:S(2)}, u32[]{:S(2)}) async-start(bf16[16,24,96]{2,1,0:T(8,128)(2,1)} %broadcast_in_dim.12), calls=%async_computation | async-start | bytes 196608 | tf_op jit(solution)/shard_map/all_to_all | solution.py:447
  13.1 2.1 %maximum_bitcast_fusion = bf16[18,2,2,12,384]{4,2,0,3,1:T(2,128)(2,1)S(1)} fusion(bf16[1,2,12,18,384]{4,1,3,2,0:T(2,128)(2,1)} %bitcast.26, bf16[1,2,12,18,384]{4,1,3,2,0:T(2,128)(2,1)} %bitcast.27), kind=kLoop, calls=%fused_computation.3 | loop fusion | flops 331776 | bytes 1327104 | tf_op jit(solution)/shard_map/transpose | solution.py:470
  15.2 1.1 %fusion.3 = (bf16[15,2,2,6,384]{4,2,0,3,1:T(2,128)(2,1)S(1)}, bf16[15,2,2,6,384]{4,2,0,3,1:T(2,128)(2,1)}) fusion(bf16[18,2,2,12,384]{4,2,0,3,1:T(2,128)(2,1)S(1)} %maximum_bitcast_fusion), kind=kLoop, calls=%fused_computation.12 | loop fusion | bytes 1105920 | tf_op jit(solution)/shard_map/slice | solution.py:477
  16.4 6.8 %all-to-all-done.x_ref = bf16[16,24,96]{2,1,0:T(8,128)(2,1)S(1)} async-done(((bf16[16,24,96]{2,1,0:T(8,128)(2,1)}), bf16[16,24,96]{2,1,0:T(8,128)(2,1)S(1)}, u32[]{:S(2)}, u32[]{:S(2)}) %all-to-all-start) | async-done | bytes 73760 | tf_op jit(solution)/shard_map/all_to_all | solution.py:447
  23.2 0.9 turn_weights.1
  24.1 4.9 %all-to-all-start.1 = ((bf16[8,96,384]{2,1,0:T(8,128)(2,1)}), bf16[8,96,384]{2,1,0:T(8,128)(2,1)}, u32[]{:S(2)}, u32[]{:S(2)}) async-start(bf16[8,96,384]{2,1,0:T(8,128)(2,1)} %turn_weights.1), calls=%async_computation.1 | async-start | bytes 1179648 | tf_op jit(solution)/shard_map/all_to_all | solution.py:453
  29.1 2.1 %collective-permute-start = (bf16[15,2,2,6,384]{4,2,0,3,1:T(2,128)(2,1)S(1)}, bf16[15,2,2,6,384]{4,2,0,3,1:T(2,128)(2,1)S(1)}, u32[]{:S(2)}, u32[]{:S(2)}) collective-permute-start(bf16[15,2,2,6,384]{4,2,0,3,1:T(2,128)(2,1)S(1)} %get-tuple-element.41), channel_id=1, source_target_pairs={{0,240},{16,0},{32,16},{48,32},{64,48},{80,64},{96,80},{112,96},{1... | collective-permute-start | bytes 829448 | tf_op jit(solution)/shard_map/ppermute | solution.py:435
  31.4 3.2 %collective-permute-done.1 = bf16[3,2,2,6,384]{4,2,0,3,1:T(2,128)(2,1)S(1)} collective-permute-done((bf16[3,2,2,6,384]{4,2,0,3,1:T(2,128)(2,1)S(1)}, bf16[3,2,2,6,384]{4,2,0,3,1:T(2,128)(2,1)S(1)}, u32[]{:S(2)}, u32[]{:S(2)}) %collective-permute-start.1) | collective-permute-done | bytes 55328 | tf_op jit(solution)/shard_map/ppermute | solution.py:437
  34.6 2.0 %collective-permute-done.2 = bf16[3,2,2,6,384]{4,2,0,3,1:T(2,128)(2,1)S(1)} collective-permute-done((bf16[3,2,2,6,384]{4,2,0,3,1:T(2,128)(2,1)S(1)}, bf16[3,2,2,6,384]{4,2,0,3,1:T(2,128)(2,1)S(1)}, u32[]{:S(2)}, u32[]{:S(2)}) %collective-permute-start.2) | collective-permute-done | bytes 55328 | tf_op jit(solution)/shard_map/ppermute | solution.py:443
  37.3 1.0 copy-done.2
  38.3 4.9 %make_bias.1.bias_ref = f32[12,144,432]{2,1,0:T(8,128)S(1)} custom-call(s32[1]{0:T(128)} %bitcast.4.last_ref, f32[12,6336]{1,0:T(8,128)S(1)} %bitcast.24, bf16[512,384]{1,0:T(8,128)(2,1)S(1)} %copy-done.2), custom_call_target="tpu_custom_call" | custom-call | tf_op jit(solution)/shard_map/make_bias/pallas_call | solution.py:91
  43.2 1.2 %collective-permute-start.3 = (bf16[8,96,384]{2,1,0:T(8,128)(2,1)}, bf16[8,96,384]{2,1,0:T(8,128)(2,1)}, u32[]{:S(2)}, u32[]{:S(2)}) collective-permute-start(bf16[8,96,384]{2,1,0:T(8,128)(2,1)} %all-to-all-done.1.w_same_ref), channel_id=1, source_target_pairs={{0,1},{1,0},{2,3},{3,2},{4,5},{5,4},{6,7},{7,6},{8,9},{9,8},{10,11... | collective-permute-start | bytes 1769480 | tf_op jit(solution)/shard_map/ppermute | solution.py:429
  44.5 2.0 %maximum_maximum_fusion = bf16[18,2,2,12,384]{4,2,0,3,1:T(2,128)(2,1)S(1)} fusion(bf16[3,2,2,6,384]{4,2,0,3,1:T(2,128)(2,1)} %copy-done.15, bf16[3,2,2,6,384]{4,2,0,3,1:T(2,128)(2,1)} %copy-done.14, bf16[15,2,2,6,384]{4,2,0,3,1:T(2,128)(2,1)} %copy-done.13, bf16[15,2,2,6,384]{4,2,0,3,1:T(2,128)(2,1)} %get-tuple-element.44), kind=kLoop, calls=%fused_computation.4 | loop fusion | flops 995328 | bytes 1327104 | tf_op jit(solution)/shard_map/concatenate | solution.py:488
  46.5 1.2 %fusion.1 = (bf16[18,1,2,12,384]{4,2,0,3,1:T(2,128)(2,1)S(1)}, bf16[18,1,2,12,384]{4,2,0,3,1:T(2,128)(2,1)}) fusion(bf16[18,2,2,12,384]{4,2,0,3,1:T(2,128)(2,1)S(1)} %maximum_maximum_fusion), kind=kLoop, calls=%fused_computation.10 | loop fusion | bytes 1327104 | tf_op jit(solution)/shard_map/slice | solution.py:492
  48.5 1.8 %reshape_squeeze.7.c_ref = bf16[432,384]{1,0:T(8,128)(2,1)} reshape(bf16[18,1,2,12,384]{4,3,2,0,1:T(8,128)(2,1)} %copy.26) | data formatting | bytes 663552 | tf_op jit(solution)/shard_map/reshape;squeeze | solution.py:492
  50.3 1.8 %copy.25 = bf16[18,1,2,12,384]{4,3,2,0,1:T(8,128)(2,1)} copy(bf16[18,1,2,12,384]{4,2,0,3,1:T(2,128)(2,1)} %get-tuple-element.88) | data formatting | bytes 663552 | tf_op jit(solution)/shard_map/slice | solution.py:491
  52.1 1.8 %reshape_squeeze.6.x_ref = bf16[432,384]{1,0:T(8,128)(2,1)} reshape(bf16[18,1,2,12,384]{4,3,2,0,1:T(8,128)(2,1)} %copy.25) | data formatting | bytes 663552 | tf_op jit(solution)/shard_map/reshape;squeeze | solution.py:491
  53.9 1.0 copy-done
  54.9 1.0 copy-done.3
  55.9 1.0 copy-done.4
  56.9 11.7 %window_block.1 = (bf16[8,112,384]{2,1,0:T(8,128)(2,1)S(1)}, bf16[8,112,384]{2,1,0:T(8,128)(2,1)S(1)}, bf16[12,32,432]{2,1,0:T(8,128)(2,1)S(1)}, bf16[12,96,144]...) custom-call(s32[1]{0:T(128)} %bitcast.me_ref, bf16[432,384]{1,0:T(8,128)(2,1)S(1)} %copy-done, bf16[432,384]{1,0:T(8,128)(2,1)S(1)} %copy-done.4, ...), custom_call_target="tpu_custom_call" | custom-call | tf_op jit(solution)/shard_map/window_block/pallas_call | solution.py:302
  68.8 2.1 %collective-permute-done.4 = bf16[8,112,384]{2,1,0:T(8,128)(2,1)S(1)} collective-permute-done((bf16[8,112,384]{2,1,0:T(8,128)(2,1)S(1)}, bf16[8,112,384]{2,1,0:T(8,128)(2,1)S(1)}, u32[]{:S(2)}, u32[]{:S(2)}) %collective-permute-start.4) | collective-permute-done | bytes 688160 | tf_op jit(solution)/shard_map/ppermute | solution.py:429
  70.9 1.0 add_convert_fusion
  71.9 5.7 %all-to-all-start.2 = ((bf16[8,112,384]{2,1,0:T(8,128)(2,1)}), bf16[8,112,384]{2,1,0:T(8,128)(2,1)S(1)}, u32[]{:S(2)}, u32[]{:S(2)}) async-start(bf16[8,112,384]{2,1,0:T(8,128)(2,1)} %add_convert_fusion), calls=%async_computation.2 | async-start | bytes 1376256 | tf_op jit(solution)/shard_map/all_to_all | solution.py:453
  77.7 1.0 copy-done.10
  78.7 2.4 %input_gradient.1 = bf16[432,384]{1,0:T(8,128)(2,1)S(1)} custom-call(s32[1]{0:T(128)} %bitcast.me_ref, bf16[432,384]{1,0:T(8,128)(2,1)S(1)} %copy-done.1, f32[1,384]{1,0:T(1,128)S(1)} %broadcast_in_dim.13.gain_ref, bf16[8,96,384]{2,1,0:T(8,128)(2,1)} %all-to-all-done.1.w_same_ref, bf16[8,96,384]{2,1,0:T(8,128)(2,1)} %collective-permute-done.3.w_other_ref, ...), custom_call_target="tpu_custom_call" | custom-call | tf_op jit(solution)/shard_map/input_gradient/pallas_call | solution.py:350
  81.3 1.0 collective-permute-start.6
  82.4 1.8 %collective-permute-start.5 = (bf16[3,2,6,384]{3,2,1,0:T(8,128)(2,1)S(1)}, bf16[3,2,6,384]{3,2,1,0:T(8,128)(2,1)S(1)}, u32[]{:S(2)}, u32[]{:S(2)}) collective-permute-start(bf16[3,2,6,384]{3,2,1,0:T(8,128)(2,1)S(1)} %get-tuple-element.94), channel_id=1, source_target_pairs={{0,1},{1,2},{2,3},{3,4},{4,5},{5,6},{6,7},{7,8},{8,9},{9,10},{10,1... | collective-permute-start | bytes 82952 | tf_op jit(solution)/shard_map/ppermute | solution.py:437
  84.2 3.5 %all-to-all-done.2.x_ref = bf16[8,112,384]{2,1,0:T(8,128)(2,1)S(1)} async-done(((bf16[8,112,384]{2,1,0:T(8,128)(2,1)}), bf16[8,112,384]{2,1,0:T(8,128)(2,1)S(1)}, u32[]{:S(2)}, u32[]{:S(2)}) %all-to-all-start.2) | async-done | bytes 688160 | tf_op jit(solution)/shard_map/all_to_all | solution.py:453
  88.6 8.9 %all-to-all-start.3 = ((bf16[16,32,96]{2,1,0:T(8,128)(2,1)}), bf16[16,32,96]{2,1,0:T(8,128)(2,1)S(1)}, u32[]{:S(2)}, u32[]{:S(2)}) async-start(bf16[16,32,96]{2,1,0:T(8,128)(2,1)} %get-tuple-element.62), calls=%async_computation.3 | async-start | bytes 262144 | tf_op jit(solution)/shard_map/all_to_all | solution.py:447
  98.4 1.0 copy.27
  99.4 8.2 %all-to-all-done.3.x_ref = bf16[16,32,96]{2,1,0:T(8,128)(2,1)S(1)} async-done(((bf16[16,32,96]{2,1,0:T(8,128)(2,1)}), bf16[16,32,96]{2,1,0:T(8,128)(2,1)S(1)}, u32[]{:S(2)}, u32[]{:S(2)}) %all-to-all-start.3) | async-done | bytes 98336 | tf_op jit(solution)/shard_map/all_to_all | solution.py:447
  (57 shorter events, 6.2 us)
Async XLA Ops:
  2.1 21.1 %all-to-all-start = ((bf16[16,24,96]{2,1,0:T(8,128)(2,1)}), bf16[16,24,96]{2,1,0:T(8,128)(2,1)S(1)}, u32[]{:S(2)}, u32[]{:S(2)}) async-start(bf16[16,24,96]{2,1,0:T(8,128)(2,1)} %broadcast_in_dim.12), calls=%async_computation | async-start | bytes 196608 | tf_op jit(solution)/shard_map/all_to_all | solution.py:447
  15.2 16.1 %copy-start.12 = (f32[1,12,6336]{2,0,1:T(1,128)S(1)}, f32[1,12,6336]{2,0,1:T(1,128)}, u32[]{:S(2)}) copy-start(f32[1,12,6336]{2,0,1:T(1,128)} %param.16) | copy-start | bytes 912388
  24.1 19.1 %all-to-all-start.1 = ((bf16[8,96,384]{2,1,0:T(8,128)(2,1)}), bf16[8,96,384]{2,1,0:T(8,128)(2,1)}, u32[]{:S(2)}, u32[]{:S(2)}) async-start(bf16[8,96,384]{2,1,0:T(8,128)(2,1)} %turn_weights.1), calls=%async_computation.1 | async-start | bytes 1179648 | tf_op jit(solution)/shard_map/all_to_all | solution.py:453
  29.1 7.5 %collective-permute-start = (bf16[15,2,2,6,384]{4,2,0,3,1:T(2,128)(2,1)S(1)}, bf16[15,2,2,6,384]{4,2,0,3,1:T(2,128)(2,1)S(1)}, u32[]{:S(2)}, u32[]{:S(2)}) collective-permute-start(bf16[15,2,2,6,384]{4,2,0,3,1:T(2,128)(2,1)S(1)} %get-tuple-element.41), channel_id=1, source_target_pairs={{0,240},{16,0},{32,16},{48,32},{64,48},{80,64},{96,80},{112,96},{1... | collective-permute-start | bytes 829448 | tf_op jit(solution)/shard_map/ppermute | solution.py:435
  31.2 3.4 %collective-permute-start.1 = (bf16[3,2,2,6,384]{4,2,0,3,1:T(2,128)(2,1)S(1)}, bf16[3,2,2,6,384]{4,2,0,3,1:T(2,128)(2,1)S(1)}, u32[]{:S(2)}, u32[]{:S(2)}) collective-permute-start(bf16[3,2,2,6,384]{4,2,0,3,1:T(2,128)(2,1)S(1)} %get-tuple-element.42), channel_id=1, source_target_pairs={{0,15},{1,0},{2,1},{3,2},{4,3},{5,4},{6,5},{7,6},{8,7},{9,8},{10,9... | collective-permute-start | bytes 165896 | tf_op jit(solution)/shard_map/ppermute | solution.py:437
  31.2 5.4 %collective-permute-start.2 = (bf16[3,2,2,6,384]{4,2,0,3,1:T(2,128)(2,1)S(1)}, bf16[3,2,2,6,384]{4,2,0,3,1:T(2,128)(2,1)S(1)}, u32[]{:S(2)}, u32[]{:S(2)}) collective-permute-start(bf16[3,2,2,6,384]{4,2,0,3,1:T(2,128)(2,1)S(1)} %get-tuple-element.43), channel_id=1, source_target_pairs={{0,255},{1,240},{2,241},{3,242},{4,243},{5,244},{6,245},{7,246},{8... | collective-permute-start | bytes 165896 | tf_op jit(solution)/shard_map/ppermute | solution.py:443
  34.6 2.0 %copy-start.14 = (bf16[3,2,2,6,384]{4,2,0,3,1:T(2,128)(2,1)}, bf16[3,2,2,6,384]{4,2,0,3,1:T(2,128)(2,1)S(1)}, u32[]{:S(2)}) copy-start(bf16[3,2,2,6,384]{4,2,0,3,1:T(2,128)(2,1)S(1)} %collective-permute-done.1) | copy-start | bytes 165892
  36.6 0.6 copy-start.15
  36.6 0.7 copy-start.13
  37.3 1.0 copy-start.2
  38.3 6.2 %copy-start.16 = (f32[384]{0:T(512)S(1)}, f32[384]{0:T(512)}, u32[]{:S(2)}) copy-start(f32[384]{0:T(512)} %param.11) | copy-start | bytes 4612
  43.2 10.7 %collective-permute-start.3 = (bf16[8,96,384]{2,1,0:T(8,128)(2,1)}, bf16[8,96,384]{2,1,0:T(8,128)(2,1)}, u32[]{:S(2)}, u32[]{:S(2)}) collective-permute-start(bf16[8,96,384]{2,1,0:T(8,128)(2,1)} %all-to-all-done.1.w_same_ref), channel_id=1, source_target_pairs={{0,1},{1,0},{2,3},{3,2},{4,5},{5,4},{6,7},{7,6},{8,9},{9,8},{10,11... | collective-permute-start | bytes 1769480 | tf_op jit(solution)/shard_map/ppermute | solution.py:429
  53.9 1.0 copy-start
  54.9 1.0 copy-start.3
  55.9 1.0 copy-start.4
  68.6 3.3 %copy-start.5 = (bf16[12,96,144]{2,1,0:T(8,128)(2,1)}, bf16[12,96,144]{2,1,0:T(8,128)(2,1)S(1)}, u32[]{:S(2)}) copy-start(bf16[12,96,144]{2,1,0:T(8,128)(2,1)S(1)} %get-tuple-element.58.dk_ref) | copy-start | bytes 995332
  68.6 3.3 %copy-start.7 = (bf16[12,96,144]{2,1,0:T(8,128)(2,1)}, bf16[12,96,144]{2,1,0:T(8,128)(2,1)S(1)}, u32[]{:S(2)}) copy-start(bf16[12,96,144]{2,1,0:T(8,128)(2,1)S(1)} %get-tuple-element.59.dv_ref) | copy-start | bytes 995332
  68.6 3.3 %copy-start.9 = (bf16[12,32,432]{2,1,0:T(8,128)(2,1)}, bf16[12,32,432]{2,1,0:T(8,128)(2,1)S(1)}, u32[]{:S(2)}) copy-start(bf16[12,32,432]{2,1,0:T(8,128)(2,1)S(1)} %get-tuple-element.57.dq_ref) | copy-start | bytes 995332
  68.6 2.2 %collective-permute-start.4 = (bf16[8,112,384]{2,1,0:T(8,128)(2,1)S(1)}, bf16[8,112,384]{2,1,0:T(8,128)(2,1)S(1)}, u32[]{:S(2)}, u32[]{:S(2)}) collective-permute-start(bf16[8,112,384]{2,1,0:T(8,128)(2,1)S(1)} %get-tuple-element.53), channel_id=1, source_target_pairs={{0,1},{1,0},{2,3},{3,2},{4,5},{5,4},{6,7},{7,6},{8,9},{9,8},{10,11... | collective-permute-start | bytes 2064392 | tf_op jit(solution)/shard_map/ppermute | solution.py:429
  70.9 6.8 %copy-start.1 = (bf16[432,384]{1,0:T(8,128)(2,1)S(1)}, bf16[432,384]{1,0:T(8,128)(2,1)}, u32[]{:S(2)}) copy-start(bf16[432,384]{1,0:T(8,128)(2,1)} %reshape_squeeze.6.x_ref) | copy-start | bytes 995332
  71.9 5.7 %copy-start.6 = (bf16[12,96,144]{2,1,0:T(8,128)(2,1)S(1)}, bf16[12,96,144]{2,1,0:T(8,128)(2,1)}, u32[]{:S(2)}) copy-start(bf16[12,96,144]{2,1,0:T(8,128)(2,1)} %copy-done.5) | copy-start | bytes 995332
  71.9 5.7 %copy-start.8 = (bf16[12,96,144]{2,1,0:T(8,128)(2,1)S(1)}, bf16[12,96,144]{2,1,0:T(8,128)(2,1)}, u32[]{:S(2)}) copy-start(bf16[12,96,144]{2,1,0:T(8,128)(2,1)} %copy-done.7) | copy-start | bytes 995332
  71.9 15.8 %all-to-all-start.2 = ((bf16[8,112,384]{2,1,0:T(8,128)(2,1)}), bf16[8,112,384]{2,1,0:T(8,128)(2,1)S(1)}, u32[]{:S(2)}, u32[]{:S(2)}) async-start(bf16[8,112,384]{2,1,0:T(8,128)(2,1)} %add_convert_fusion), calls=%async_computation.2 | async-start | bytes 1376256 | tf_op jit(solution)/shard_map/all_to_all | solution.py:453
  77.7 1.0 copy-start.10
  81.1 17.1 %copy-start.11 = (bf16[2,12,18,384]{3,0,2,1:T(2,128)(2,1)S(1)}, bf16[2,12,18,384]{3,0,2,1:T(2,128)(2,1)}, u32[]{:S(2)}) copy-start(bf16[2,12,18,384]{3,0,2,1:T(2,128)(2,1)} %param.10) | copy-start | bytes 995332
  81.3 16.2 %collective-permute-start.6 = (bf16[15,2,6,384]{3,2,1,0:T(8,128)(2,1)S(1)}, bf16[15,2,6,384]{3,2,1,0:T(8,128)(2,1)S(1)}, u32[]{:S(2)}, u32[]{:S(2)}) collective-permute-start(bf16[15,2,6,384]{3,2,1,0:T(8,128)(2,1)S(1)} %slice.59), channel_id=1, source_target_pairs={{0,16},{16,32},{32,48},{48,64},{64,80},{80,96},{96,112},{112,128},... | collective-permute-start | bytes 414728 | tf_op jit(solution)/shard_map/ppermute | solution.py:435
  82.3 15.2 %collective-permute-start.7 = (bf16[3,2,6,384]{3,2,1,0:T(8,128)(2,1)S(1)}, bf16[3,2,6,384]{3,2,1,0:T(8,128)(2,1)S(1)}, u32[]{:S(2)}, u32[]{:S(2)}) collective-permute-start(bf16[3,2,6,384]{3,2,1,0:T(8,128)(2,1)S(1)} %get-tuple-element.93), channel_id=1, source_target_pairs={{0,17},{1,18},{2,19},{3,20},{4,21},{5,22},{6,23},{7,24},{8,25},{9,... | collective-permute-start | bytes 82952 | tf_op jit(solution)/shard_map/ppermute | solution.py:443
  82.4 15.1 %collective-permute-start.5 = (bf16[3,2,6,384]{3,2,1,0:T(8,128)(2,1)S(1)}, bf16[3,2,6,384]{3,2,1,0:T(8,128)(2,1)S(1)}, u32[]{:S(2)}, u32[]{:S(2)}) collective-permute-start(bf16[3,2,6,384]{3,2,1,0:T(8,128)(2,1)S(1)} %get-tuple-element.94), channel_id=1, source_target_pairs={{0,1},{1,2},{2,3},{3,4},{4,5},{5,6},{6,7},{7,8},{8,9},{9,10},{10,1... | collective-permute-start | bytes 82952 | tf_op jit(solution)/shard_map/ppermute | solution.py:437
  88.6 19.0 %all-to-all-start.3 = ((bf16[16,32,96]{2,1,0:T(8,128)(2,1)}), bf16[16,32,96]{2,1,0:T(8,128)(2,1)S(1)}, u32[]{:S(2)}, u32[]{:S(2)}) async-start(bf16[16,32,96]{2,1,0:T(8,128)(2,1)} %get-tuple-element.62), calls=%async_computation.3 | async-start | bytes 262144 | tf_op jit(solution)/shard_map/all_to_all | solution.py:447
where the time goes:
time: 109 us; the launch traced here: 108 us
  starting transfers between devices  37.1 us (34%)
  waiting for transfers between devices  25.7 us (24%)
  Pallas kernels  21.6 us (20%)
  local copies, waits for them, and re-layouts  16.8 us (15%)
  other arithmetic  6.15 us (6%)
    all_to_all x2, starting transfers between devices, spread_over_lat(): return lax.all_to_all(x, 'lat', 0, 0)  19.9 us
    all_to_all x2, waiting for transfers between devices, spread_over_lat(): return lax.all_to_all(x, 'lat', 0, 0)  15 us
    pallas_call x1, Pallas kernels, run_block(): pl.pallas_call(functools.partial(block_kernel, heads=heads, windows=windo...  11.7 us
    all_to_all x2, starting transfers between devices, spread_over_lon(): return lax.all_to_all(x, 'lon', 0, 0, axis_index_groups=groups)  10.6 us
    unnamed x37, local copies, waits for them, and re-layouts  7.35 us
    pallas_call x1, Pallas kernels, make_bias(): pl.pallas_call(functools.partial(bias_kernel, levels=levels, lat_rows=lat...  4.92 us
    all_to_all x2, waiting for transfers between devices, spread_over_lon(): return lax.all_to_all(x, 'lon', 0, 0, axis_index_groups=groups)  3.49 us
    ppermute x2, waiting for transfers between devices, shift(): lax.ppermute(x, 'lon', [(i, (i + lon_by) % lons) for i in range(lons)])  3.19 us
  transfers between devices with their start and end apart: 12, of which 6 were waited for; matrix products, arithmetic and copies ran while one was open for 14% of the time, Pallas kernels for 8%

commit v1 on v0

--- a/solution.py
+++ b/solution.py
@@ -13,7 +13,7 @@
 MASKED = -1000000000.0
 LOG2E = math.log2(math.e)
 UNROLL = 6
-BLOCK_MB = 28
+BLOCK_MB = 48
 SMALL_MB = 16
 F32 = jnp.float32
 BF16 = jnp.bfloat16
@@ -472,31 +472,24 @@
     mine = jnp.concatenate([w_query, w_key, w_value, w_out], axis=1)
     rows_all = spread_over_lat(jnp.broadcast_to(mine[None], (lats,) + mine.shape))
     turned = turn(rows_all, lons // 2)
-    pieces = (
-        both[half_cols:, :, :, half_rows:],
-        both[half_cols:, :, :, :half_rows],
-        both[:half_cols, :, :, half_rows:],
-        both[:half_cols, :, :, :half_rows],
-    )
-    turned, pieces = lax.optimization_barrier((turned, pieces))
+    turned, table = lax.optimization_barrier((turned, rel_table[0]))
     w_same = spread_over_lon(turned)
-    own = pieces[0]
-    south = shift(pieces[1], -1, 0)
-    east = shift(pieces[2], 0, -1)
-    corner = shift(pieces[3], -1, -1)
-    own, south, east, corner, table = lax.optimization_barrier((own, south, east, corner, rel_table[0]))
+    own = both[half_cols:, :, :, half_rows:]
+    south = shift(both[half_cols:, :, :, :half_rows], -1, 0)
+    east = shift(both[:half_cols, :, :, half_rows:], 0, -1)
+    corner = shift(both[:half_cols, :, :, :half_rows], -1, -1)
+
+    order = jnp.asarray(offset_order(rels, levels, lat_rows, 256), BF16)
+    last = (me_lat == lats - 1).astype(jnp.int32).reshape(1)
+    slots = heads + -heads % 16
+    bias = make_bias(last, table, order, levels, lat_rows, rels, slots, windows)
+    w_same, bias, own, south, east, corner = lax.optimization_barrier((w_same, bias, own, south, east, corner))
+    w_other = swap(w_same, "lon", 1)
     moved = jnp.concatenate(
         [jnp.concatenate([own, south], axis=3), jnp.concatenate([east, corner], axis=3)], axis=0
     )
     shifted = moved[:, 0].reshape(-1, feat)
     cot_shift = moved[:, 1].reshape(-1, feat)
-
-    order = jnp.asarray(offset_order(rels, levels, lat_rows, 256), BF16)
-    last = (me_lat == lats - 1).astype(jnp.int32).reshape(1)
-    slots = heads + -heads % 16
-    bias = make_bias(last, table, order, levels, lat_rows, rels, slots, windows)
-    w_same, bias = lax.optimization_barrier((w_same, bias))
-    w_other = swap(w_same, "lon", 1)
 
     me = me_lon.reshape(1)
     gain = norm_gain[None]

time: 109 us -> 95.7 us (0.88)
  local copies, waits for them, and re-layouts: 16.8 us -> 7.47 us
  starting transfers between devices: 37.1 us -> 34.2 us
    all_to_all x2, waiting for transfers between devices: 3.49 us -> 9.16 us  [spread_over_lon(): return lax.all_to_all(x, 'lon', 0, 0, axis_index_groups=groups)]
    all_to_all x2, starting transfers between devices: 19.9 us -> 15.7 us  [spread_over_lat(): return lax.all_to_all(x, 'lat', 0, 0)]
    ppermute x2, waiting for transfers between devices: 3.19 us -> 0.01 us  [shift(): lax.ppermute(x, 'lon', [(i, (i + lon_by) % lons) for i in range(lons)])]
    ppermute x2, waiting for transfers between devices: 1.98 us -> 0.01 us  [shift(): return lax.ppermute(x, ('lat', 'lon'), pairs)]
    unnamed x37 -> x15, local copies, waits for them, and re-layouts: 7.35 us -> 5.43 us
    another operation x1, local copies, waits for them, and re-layouts: 1.82 us -> 0.08 us  [local(): cot_shift = moved[:, 1].reshape(-1, feat)]
    slice x1, local copies, waits for them, and re-layouts: 1.8 us -> 0.06 us  [local(): shifted = moved[:, 0].reshape(-1, feat)]
    another operation x1, local copies, waits for them, and re-layouts: 1.81 us -> 0.08 us  [local(): shifted = moved[:, 0].reshape(-1, feat)]
  transfers between devices with their start and end apart: 12 -> 12, of which waited for: 6 -> 4; matrix products, arithmetic and copies ran while one was open for 14% -> 8% of each run, Pallas kernels for 8% -> 7%
where the time goes in v1:
time: 95.7 us; the launch traced here: 95.1 us
  starting transfers between devices  34.2 us (36%)
  waiting for transfers between devices  26.2 us (27%)
  Pallas kernels  21.2 us (22%)
  local copies, waits for them, and re-layouts  7.47 us (8%)
  other arithmetic  5.13 us (5%)
    all_to_all x2, starting transfers between devices, spread_over_lat(): return lax.all_to_all(x, 'lat', 0, 0)  15.7 us
    all_to_all x2, waiting for transfers between devices, spread_over_lat(): return lax.all_to_all(x, 'lat', 0, 0)  15.1 us
    pallas_call x1, Pallas kernels, run_block(): pl.pallas_call(functools.partial(block_kernel, heads=heads, windows=windo...  12.5 us
    all_to_all x2, starting transfers between devices, spread_over_lon(): return lax.all_to_all(x, 'lon', 0, 0, axis_index_groups=groups)  11.9 us
    all_to_all x2, waiting for transfers between devices, spread_over_lon(): return lax.all_to_all(x, 'lon', 0, 0, axis_index_groups=groups)  9.16 us
    unnamed x15, local copies, waits for them, and re-layouts  5.43 us
    pallas_call x1, Pallas kernels, make_bias(): pl.pallas_call(functools.partial(bias_kernel, levels=levels, lat_rows=lat...  4.92 us
    ppermute x2, starting transfers between devices, shift(): lax.ppermute(x, 'lat', [(i, (i + lat_by) % lats) for i in range(lats)])  3.62 us
  transfers between devices with their start and end apart: 12, of which 4 were waited for; matrix products, arithmetic and copies ran while one was open for 8% of the time, Pallas kernels for 7%

profile of v1, /device:TPU:8, one launch (start us, length us, event | category | flops | bytes accessed | tf_op | source)
XLA Modules:
  0.0 95.1 jit_solution(15781982095380192636)
XLA Ops:
  0.6 0.8 pad_maximum_fusion
  1.5 0.7 broadcast_in_dim.12
  2.1 11.0 %all-to-all-start = ((bf16[16,24,96]{2,1,0:T(8,128)(2,1)}), bf16[16,24,96]{2,1,0:T(8,128)(2,1)S(1)}, u32[]{:S(2)}, u32[]{:S(2)}) async-start(bf16[16,24,96]{2,1,0:T(8,128)(2,1)} %broadcast_in_dim.12), calls=%async_computation | async-start | bytes 196608 | tf_op jit(solution)/shard_map/all_to_all | solution.py:447
  13.2 1.0 %copy.32 = f32[1,12,6336]{2,1,0:T(8,128)S(1)} copy(f32[1,12,6336]{2,0,1:T(1,128)} %param.16) | data formatting | bytes 608256
  14.2 2.1 %maximum_bitcast_fusion = bf16[18,2,2,12,384]{4,2,0,3,1:T(2,128)(2,1)S(1)} fusion(bf16[1,2,12,18,384]{4,1,3,2,0:T(2,128)(2,1)} %bitcast.26, bf16[1,2,12,18,384]{4,1,3,2,0:T(2,128)(2,1)} %bitcast.27), kind=kLoop, calls=%fused_computation.3 | loop fusion | flops 331776 | bytes 1327104 | tf_op jit(solution)/shard_map/transpose | solution.py:470
  16.2 7.0 %all-to-all-done.x_ref = bf16[16,24,96]{2,1,0:T(8,128)(2,1)S(1)} async-done(((bf16[16,24,96]{2,1,0:T(8,128)(2,1)}), bf16[16,24,96]{2,1,0:T(8,128)(2,1)S(1)}, u32[]{:S(2)}, u32[]{:S(2)}) %all-to-all-start) | async-done | bytes 73760 | tf_op jit(solution)/shard_map/all_to_all | solution.py:447
  23.2 0.9 turn_weights.1
  24.1 5.1 %all-to-all-start.1 = ((bf16[8,96,384]{2,1,0:T(8,128)(2,1)}), bf16[8,96,384]{2,1,0:T(8,128)(2,1)S(1)}, u32[]{:S(2)}, u32[]{:S(2)}) async-start(bf16[8,96,384]{2,1,0:T(8,128)(2,1)} %turn_weights.1), calls=%async_computation.1 | async-start | bytes 1179648 | tf_op jit(solution)/shard_map/all_to_all | solution.py:453
  29.2 0.4 fusion.3
  29.6 2.2 %collective-permute-start = (bf16[15,2,2,6,384]{4,2,0,3,1:T(2,128)(2,1)S(1)}, bf16[15,2,2,6,384]{4,2,0,3,1:T(2,128)(2,1)S(1)}, u32[]{:S(2)}, u32[]{:S(2)}) collective-permute-start(bf16[15,2,2,6,384]{4,2,0,3,1:T(2,128)(2,1)S(1)} %get-tuple-element.83), channel_id=1, source_target_pairs={{0,240},{16,0},{32,16},{48,32},{64,48},{80,64},{96,80},{112,96},{1... | collective-permute-start | bytes 829448 | tf_op jit(solution)/shard_map/ppermute | solution.py:435
  31.9 0.3 collective-permute-start.1
  32.3 4.9 %make_bias.1.bias_ref = f32[12,144,432]{2,1,0:T(8,128)S(1)} custom-call(s32[1]{0:T(128)} %bitcast.1.last_ref, f32[12,6336]{1,0:T(8,128)S(1)} %bitcast.24, bf16[512,384]{1,0:T(8,128)(2,1)S(1)} %copy-done.1), custom_call_target="tpu_custom_call" | custom-call | tf_op jit(solution)/shard_map/make_bias/pallas_call | solution.py:91
  37.2 1.7 %copy-done = f32[12,144,432]{2,1,0:T(8,128)} copy-done((f32[12,144,432]{2,1,0:T(8,128)}, f32[12,144,432]{2,1,0:T(8,128)S(1)}, u32[]{:S(2)}) %copy-start) | copy-done | bytes 2986008
  39.0 0.7 collective-permute-start.3
  39.6 1.0 %maximum_maximum_fusion = bf16[18,2,2,12,384]{4,2,0,3,1:T(2,128)(2,1)S(1)} fusion(bf16[3,2,2,6,384]{4,2,0,3,1:T(2,128)(2,1)S(1)} %collective-permute-done.2, bf16[3,2,2,6,384]{4,2,0,3,1:T(2,128)(2,1)S(1)} %collective-permute-done.1, bf16[15,2,2,6,384]{4,2,0,3,1:T(2,128)(2,1)S(1)} %collective-permute-done, bf16[15,2,2,6,384]{4,2,0,3,1:T(2,128)(2,1)S(1)} %get-tuple-element.38), kind=kLoop, calls=%fused_computation.4 | loop fusion | flops 995328 | bytes 1327104 | tf_op jit(solution)/shard_map/concatenate | solution.py:488
  40.6 0.5 fusion.1
  41.4 12.5 %window_block.1 = (bf16[8,112,384]{2,1,0:T(8,128)(2,1)S(1)}, bf16[8,112,384]{2,1,0:T(8,128)(2,1)S(1)}, bf16[12,32,432]{2,1,0:T(8,128)(2,1)S(1)}, bf16[12,96,144]...) custom-call(s32[1]{0:T(128)} %bitcast.me_ref, bf16[432,384]{1,0:T(8,128)(2,1)S(1)} %reshape_squeeze.6.x_ref, ...), custom_call_target="tpu_custom_call" | custom-call | tf_op jit(solution)/shard_map/window_block/pallas_call | solution.py:302
  54.0 0.3 collective-permute-start.4
  54.3 1.9 %collective-permute-done.4 = bf16[8,112,384]{2,1,0:T(8,128)(2,1)S(1)} collective-permute-done((bf16[8,112,384]{2,1,0:T(8,128)(2,1)S(1)}, bf16[8,112,384]{2,1,0:T(8,128)(2,1)S(1)}, u32[]{:S(2)}, u32[]{:S(2)}) %collective-permute-start.4) | collective-permute-done | bytes 688160 | tf_op jit(solution)/shard_map/ppermute | solution.py:429
  56.2 1.1 %add_convert_fusion = bf16[8,112,384]{2,1,0:T(8,128)(2,1)} fusion(bf16[8,112,384]{2,1,0:T(8,128)(2,1)S(1)} %collective-permute-done.4, bf16[8,112,384]{2,1,0:T(8,128)(2,1)S(1)} %get-tuple-element.44), kind=kLoop, calls=%fused_computation | loop fusion | flops 1376256 | bytes 2064384 | tf_op jit(solution)/shard_map/convert_element_type | solution.py:500
  57.3 6.8 %all-to-all-start.2 = ((bf16[8,112,384]{2,1,0:T(8,128)(2,1)}), bf16[8,112,384]{2,1,0:T(8,128)(2,1)S(1)}, u32[]{:S(2)}, u32[]{:S(2)}) async-start(bf16[8,112,384]{2,1,0:T(8,128)(2,1)} %add_convert_fusion), calls=%async_computation.2 | async-start | bytes 1376256 | tf_op jit(solution)/shard_map/all_to_all | solution.py:453
  64.0 1.1 %copy-done.3 = bf16[12,96,144]{2,1,0:T(8,128)(2,1)S(1)} copy-done((bf16[12,96,144]{2,1,0:T(8,128)(2,1)S(1)}, bf16[12,96,144]{2,1,0:T(8,128)(2,1)}, u32[]{:S(2)}) %copy-start.3) | copy-done | bytes 331800
  65.1 1.2 %input_gradient.1 = bf16[432,384]{1,0:T(8,128)(2,1)S(1)} custom-call(s32[1]{0:T(128)} %bitcast.me_ref, bf16[432,384]{1,0:T(8,128)(2,1)S(1)} %reshape_squeeze.6.x_ref, f32[1,384]{1,0:T(1,128)S(1)} %broadcast_in_dim.13.gain_ref, bf16[8,96,384]{2,1,0:T(8,128)(2,1)S(1)} %all-to-all-done.1.w_same_ref, bf16[8,96,384]{2,1,0:T(8,128)(2,1)S(1)} %collective-permute-done.3.w_other_ref, ...), custom_call_target="tpu_custom_call" | custom-call | tf_op jit(solution)/shard_map/input_gradient/pallas_call | solution.py:350
  66.5 1.5 %collective-permute-start.6 = (bf16[15,2,6,384]{3,2,1,0:T(8,128)(2,1)S(1)}, bf16[15,2,6,384]{3,2,1,0:T(8,128)(2,1)S(1)}, u32[]{:S(2)}, u32[]{:S(2)}) collective-permute-start(bf16[15,2,6,384]{3,2,1,0:T(8,128)(2,1)S(1)} %slice.59), channel_id=1, source_target_pairs={{0,16},{16,32},{32,48},{48,64},{64,80},{80,96},{96,112},{112,128},... | collective-permute-start | bytes 414728 | tf_op jit(solution)/shard_map/ppermute | solution.py:435
  68.0 1.6 %collective-permute-start.5 = (bf16[3,2,6,384]{3,2,1,0:T(8,128)(2,1)S(1)}, bf16[3,2,6,384]{3,2,1,0:T(8,128)(2,1)S(1)}, u32[]{:S(2)}, u32[]{:S(2)}) collective-permute-start(bf16[3,2,6,384]{3,2,1,0:T(8,128)(2,1)S(1)} %get-tuple-element.86), channel_id=1, source_target_pairs={{0,1},{1,2},{2,3},{3,4},{4,5},{5,6},{6,7},{7,8},{8,9},{9,10},{10,1... | collective-permute-start | bytes 82952 | tf_op jit(solution)/shard_map/ppermute | solution.py:437
  69.6 9.2 %all-to-all-done.2.x_ref = bf16[8,112,384]{2,1,0:T(8,128)(2,1)S(1)} async-done(((bf16[8,112,384]{2,1,0:T(8,128)(2,1)}), bf16[8,112,384]{2,1,0:T(8,128)(2,1)S(1)}, u32[]{:S(2)}, u32[]{:S(2)}) %all-to-all-start.2) | async-done | bytes 688160 | tf_op jit(solution)/shard_map/all_to_all | solution.py:453
  78.8 0.9 sum_and_turn.1
  79.7 4.7 %all-to-all-start.3 = ((bf16[16,32,96]{2,1,0:T(8,128)(2,1)}), bf16[16,32,96]{2,1,0:T(8,128)(2,1)S(1)}, u32[]{:S(2)}, u32[]{:S(2)}) async-start(bf16[16,32,96]{2,1,0:T(8,128)(2,1)} %get-tuple-element.54), calls=%async_computation.3 | async-start | bytes 262144 | tf_op jit(solution)/shard_map/all_to_all | solution.py:447
  84.4 0.6 copy.28
  85.3 1.0 %copy.27 = bf16[2,12,18,384]{3,0,2,1:T(2,128)(2,1)} copy(bf16[2,12,18,384]{3,1,0,2:T(8,128)(2,1)S(1)} %fusion) | data formatting | bytes 663552
  86.3 8.2 %all-to-all-done.3.x_ref = bf16[16,32,96]{2,1,0:T(8,128)(2,1)S(1)} async-done(((bf16[16,32,96]{2,1,0:T(8,128)(2,1)}), bf16[16,32,96]{2,1,0:T(8,128)(2,1)S(1)}, u32[]{:S(2)}, u32[]{:S(2)}) %all-to-all-start.3) | async-done | bytes 98336 | tf_op jit(solution)/shard_map/all_to_all | solution.py:447
  94.4 0.7 last_sum.1
  (35 shorter events, 1.0 us)
Async XLA Ops:
  2.1 21.1 %all-to-all-start = ((bf16[16,24,96]{2,1,0:T(8,128)(2,1)}), bf16[16,24,96]{2,1,0:T(8,128)(2,1)S(1)}, u32[]{:S(2)}, u32[]{:S(2)}) async-start(bf16[16,24,96]{2,1,0:T(8,128)(2,1)} %broadcast_in_dim.12), calls=%async_computation | async-start | bytes 196608 | tf_op jit(solution)/shard_map/all_to_all | solution.py:447
  24.1 8.1 %copy-start.1 = (bf16[512,384]{1,0:T(8,128)(2,1)S(1)}, bf16[512,384]{1,0:T(8,128)(2,1)}, u32[]{:S(2)}) copy-start(bf16[512,384]{1,0:T(8,128)(2,1)} %constant.11.clone.order_ref) | copy-start | bytes 1179652
  24.1 14.8 %all-to-all-start.1 = ((bf16[8,96,384]{2,1,0:T(8,128)(2,1)}), bf16[8,96,384]{2,1,0:T(8,128)(2,1)S(1)}, u32[]{:S(2)}, u32[]{:S(2)}) async-start(bf16[8,96,384]{2,1,0:T(8,128)(2,1)} %turn_weights.1), calls=%async_computation.1 | async-start | bytes 1179648 | tf_op jit(solution)/shard_map/all_to_all | solution.py:453
  29.6 9.3 %collective-permute-start = (bf16[15,2,2,6,384]{4,2,0,3,1:T(2,128)(2,1)S(1)}, bf16[15,2,2,6,384]{4,2,0,3,1:T(2,128)(2,1)S(1)}, u32[]{:S(2)}, u32[]{:S(2)}) collective-permute-start(bf16[15,2,2,6,384]{4,2,0,3,1:T(2,128)(2,1)S(1)} %get-tuple-element.83), channel_id=1, source_target_pairs={{0,240},{16,0},{32,16},{48,32},{64,48},{80,64},{96,80},{112,96},{1... | collective-permute-start | bytes 829448 | tf_op jit(solution)/shard_map/ppermute | solution.py:435
  31.8 7.1 %collective-permute-start.2 = (bf16[3,2,2,6,384]{4,2,0,3,1:T(2,128)(2,1)S(1)}, bf16[3,2,2,6,384]{4,2,0,3,1:T(2,128)(2,1)S(1)}, u32[]{:S(2)}, u32[]{:S(2)}) collective-permute-start(bf16[3,2,2,6,384]{4,2,0,3,1:T(2,128)(2,1)S(1)} %get-tuple-element.81), channel_id=1, source_target_pairs={{0,255},{1,240},{2,241},{3,242},{4,243},{5,244},{6,245},{7,246},{8... | collective-permute-start | bytes 165896 | tf_op jit(solution)/shard_map/ppermute | solution.py:443
  31.9 7.0 %collective-permute-start.1 = (bf16[3,2,2,6,384]{4,2,0,3,1:T(2,128)(2,1)S(1)}, bf16[3,2,2,6,384]{4,2,0,3,1:T(2,128)(2,1)S(1)}, u32[]{:S(2)}, u32[]{:S(2)}) collective-permute-start(bf16[3,2,2,6,384]{4,2,0,3,1:T(2,128)(2,1)S(1)} %get-tuple-element.82), channel_id=1, source_target_pairs={{0,15},{1,0},{2,1},{3,2},{4,3},{5,4},{6,5},{7,6},{8,7},{9,8},{10,9... | collective-permute-start | bytes 165896 | tf_op jit(solution)/shard_map/ppermute | solution.py:437
  32.3 7.3 %copy-start.5 = (f32[384]{0:T(512)S(1)}, f32[384]{0:T(512)}, u32[]{:S(2)}) copy-start(f32[384]{0:T(512)} %param.11) | copy-start | bytes 4612
  37.2 1.7 %copy-start = (f32[12,144,432]{2,1,0:T(8,128)}, f32[12,144,432]{2,1,0:T(8,128)S(1)}, u32[]{:S(2)}) copy-start(f32[12,144,432]{2,1,0:T(8,128)S(1)} %make_bias.1.bias_ref) | copy-start | bytes 8957956
  39.0 2.4 %collective-permute-start.3 = (bf16[8,96,384]{2,1,0:T(8,128)(2,1)S(1)}, bf16[8,96,384]{2,1,0:T(8,128)(2,1)S(1)}, u32[]{:S(2)}, u32[]{:S(2)}) collective-permute-start(bf16[8,96,384]{2,1,0:T(8,128)(2,1)S(1)} %all-to-all-done.1.w_same_ref), channel_id=1, source_target_pairs={{0,1},{1,0},{2,3},{3,2},{4,5},{5,4},{6,7},{7,6},{8,9},{9,8},{10,11... | collective-permute-start | bytes 1769480 | tf_op jit(solution)/shard_map/ppermute | solution.py:429
  54.0 3.3 %copy-start.2 = (bf16[12,96,144]{2,1,0:T(8,128)(2,1)}, bf16[12,96,144]{2,1,0:T(8,128)(2,1)S(1)}, u32[]{:S(2)}) copy-start(bf16[12,96,144]{2,1,0:T(8,128)(2,1)S(1)} %get-tuple-element.51.dv_ref) | copy-start | bytes 995332
  54.0 2.2 %collective-permute-start.4 = (bf16[8,112,384]{2,1,0:T(8,128)(2,1)S(1)}, bf16[8,112,384]{2,1,0:T(8,128)(2,1)S(1)}, u32[]{:S(2)}, u32[]{:S(2)}) collective-permute-start(bf16[8,112,384]{2,1,0:T(8,128)(2,1)S(1)} %get-tuple-element.45), channel_id=1, source_target_pairs={{0,1},{1,0},{2,3},{3,2},{4,5},{5,4},{6,7},{7,6},{8,9},{9,8},{10,11... | collective-permute-start | bytes 2064392 | tf_op jit(solution)/shard_map/ppermute | solution.py:429
  57.3 21.5 %all-to-all-start.2 = ((bf16[8,112,384]{2,1,0:T(8,128)(2,1)}), bf16[8,112,384]{2,1,0:T(8,128)(2,1)S(1)}, u32[]{:S(2)}, u32[]{:S(2)}) async-start(bf16[8,112,384]{2,1,0:T(8,128)(2,1)} %add_convert_fusion), calls=%async_computation.2 | async-start | bytes 1376256 | tf_op jit(solution)/shard_map/all_to_all | solution.py:453
  64.0 1.1 %copy-start.3 = (bf16[12,96,144]{2,1,0:T(8,128)(2,1)S(1)}, bf16[12,96,144]{2,1,0:T(8,128)(2,1)}, u32[]{:S(2)}) copy-start(bf16[12,96,144]{2,1,0:T(8,128)(2,1)} %copy-done.2) | copy-start | bytes 995332
  66.3 18.8 %copy-start.4 = (bf16[2,12,18,384]{3,0,2,1:T(2,128)(2,1)S(1)}, bf16[2,12,18,384]{3,0,2,1:T(2,128)(2,1)}, u32[]{:S(2)}) copy-start(bf16[2,12,18,384]{3,0,2,1:T(2,128)(2,1)} %param.10) | copy-start | bytes 995332
  66.5 17.9 %collective-permute-start.6 = (bf16[15,2,6,384]{3,2,1,0:T(8,128)(2,1)S(1)}, bf16[15,2,6,384]{3,2,1,0:T(8,128)(2,1)S(1)}, u32[]{:S(2)}, u32[]{:S(2)}) collective-permute-start(bf16[15,2,6,384]{3,2,1,0:T(8,128)(2,1)S(1)} %slice.59), channel_id=1, source_target_pairs={{0,16},{16,32},{32,48},{48,64},{64,80},{80,96},{96,112},{112,128},... | collective-permute-start | bytes 414728 | tf_op jit(solution)/shard_map/ppermute | solution.py:435
  68.0 16.4 %collective-permute-start.7 = (bf16[3,2,6,384]{3,2,1,0:T(8,128)(2,1)S(1)}, bf16[3,2,6,384]{3,2,1,0:T(8,128)(2,1)S(1)}, u32[]{:S(2)}, u32[]{:S(2)}) collective-permute-start(bf16[3,2,6,384]{3,2,1,0:T(8,128)(2,1)S(1)} %get-tuple-element.85), channel_id=1, source_target_pairs={{0,17},{1,18},{2,19},{3,20},{4,21},{5,22},{6,23},{7,24},{8,25},{9,... | collective-permute-start | bytes 82952 | tf_op jit(solution)/shard_map/ppermute | solution.py:443
  68.0 16.3 %collective-permute-start.5 = (bf16[3,2,6,384]{3,2,1,0:T(8,128)(2,1)S(1)}, bf16[3,2,6,384]{3,2,1,0:T(8,128)(2,1)S(1)}, u32[]{:S(2)}, u32[]{:S(2)}) collective-permute-start(bf16[3,2,6,384]{3,2,1,0:T(8,128)(2,1)S(1)} %get-tuple-element.86), channel_id=1, source_target_pairs={{0,1},{1,2},{2,3},{3,4},{4,5},{5,6},{6,7},{7,8},{8,9},{9,10},{10,1... | collective-permute-start | bytes 82952 | tf_op jit(solution)/shard_map/ppermute | solution.py:437
  79.7 14.8 %all-to-all-start.3 = ((bf16[16,32,96]{2,1,0:T(8,128)(2,1)}), bf16[16,32,96]{2,1,0:T(8,128)(2,1)S(1)}, u32[]{:S(2)}, u32[]{:S(2)}) async-start(bf16[16,32,96]{2,1,0:T(8,128)(2,1)} %get-tuple-element.54), calls=%async_computation.3 | async-start | bytes 262144 | tf_op jit(solution)/shard_map/all_to_all | solution.py:447

commit v2 on v1

--- a/solution.py
+++ b/solution.py
@@ -12,7 +12,7 @@
 EPSILON = 1e-05
 MASKED = -1000000000.0
 LOG2E = math.log2(math.e)
-UNROLL = 6
+UNROLL = 12
 BLOCK_MB = 48
 SMALL_MB = 16
 F32 = jnp.float32
@@ -75,8 +75,7 @@
             off = (lon_width - 1 - p) * cell
             rolled = pltpu.roll(strip, lanes - off, 1) if off else strip
             bias_s[p * cell:(p + 1) * cell, :] = rolled[:, :tokens]
-        bias = bias_s[...].T
-        out_ref[h] = jnp.concatenate([bias] * windows, axis=1)
+        out_ref[h] = bias_s[...].T
         return carry
 
     lax.fori_loop(0, heads, head, 0)
@@ -90,7 +89,7 @@
     vmem = pl.BlockSpec(memory_space=pltpu.VMEM)
     return pl.pallas_call(
         functools.partial(bias_kernel, levels=levels, lat_rows=lat_rows, rels=rels, windows=windows),
-        out_shape=jax.ShapeDtypeStruct((heads, tokens, windows * tokens), F32),
+        out_shape=jax.ShapeDtypeStruct((heads, tokens, tokens), F32),
         in_specs=[pl.BlockSpec(memory_space=pltpu.SMEM), vmem, vmem],
         out_specs=vmem,
         scratch_shapes=[
@@ -146,7 +145,7 @@
 def block_kernel(
     me_ref, x_ref, c_ref, gain_ref, w_same_ref, w_other_ref, bias_ref, order_ref,
     same_ref, other_ref, dq_s, dk_s, dv_s,
-    w_s, gw_s, normed_s, q_s, d_s, k_s, v_s, ctx_s, dsum_s, fold_s, pick_s,
+    w_s, gw_s, normed_s, q_s, d_s, k_s, v_s, ctx_s, dsum_s, fold_s, pick_s, lines_s,
     *, heads, windows, levels, lat_rows, rels,
 ):
     feat = x_ref.shape[1]
@@ -195,7 +194,7 @@
 
     def head(h, carry):
         qh, dh, kh, vh = q_s[h], d_s[h], k_s[h], v_s[h]
-        score = mm(kh, qh, TN) * (scale * LOG2E) + bias_ref[h]
+        score = mm(kh, qh, TN) * (scale * LOG2E) + jnp.concatenate([bias_ref[h]] * windows, axis=1)
         d_prob = mm(vh, dh, TN)
         expo = jnp.exp2(score - jnp.max(score, axis=0, keepdims=True))
         prob = expo * (1.0 / jnp.sum(expo, axis=0, keepdims=True))
@@ -265,11 +264,6 @@
         )
         gains = jnp.where((row == 4 + i) & (lane >= 32) & (lane < 64), turned, gains)
 
-    for ref, side in ((same_ref, parity), (other_ref, 1 - parity)):
-        for i in range(pairs):
-            start = pl.multiple_of((2 * i + side) * part, part)
-            block = jnp.concatenate([gw_s[k, pl.ds(start, part), :] for k in range(4)], axis=0)
-            ref[i, 0:packed, :] = block.astype(BF16)
     for j in range(2 * pairs):
         z, w, a = j // (levels * per), j // per % levels, j % per
         at = (z * per + a) * slots
@@ -277,15 +271,13 @@
         tail = line[:, feat:]
         moved = jnp.concatenate([pltpu.roll(tail[:8], 4, 0), tail[:8], pltpu.roll(tail[8:], 4, 0)], axis=1)
         moved = jnp.where(lane < 32, moved, gains)
-        lines = jnp.concatenate([line[:8, :feat], jnp.where(row >= 4, moved, line[8:, :feat])], axis=0).astype(BF16)
-
-        @pl.when(parity == j % 2)
-        def _():
-            same_ref[j // 2, packed:, :] = lines
-
-        @pl.when(parity != j % 2)
-        def _():
-            other_ref[j // 2, packed:, :] = lines
+        lines_s[j] = jnp.concatenate([line[:8, :feat], jnp.where(row >= 4, moved, line[8:, :feat])], axis=0).astype(BF16)
+    for ref, side in ((same_ref, parity), (other_ref, 1 - parity)):
+        for i in range(pairs):
+            start = pl.multiple_of((2 * i + side) * part, part)
+            block = jnp.concatenate([gw_s[k, pl.ds(start, part), :] for k in range(4)], axis=0)
+            ref[i, 0:packed, :] = block.astype(BF16)
+            ref[i, packed:, :] = lines_s[2 * i + side]
 
 
 def run_block(me, x, c, gain, w_same, w_other, bias, order, heads, windows, levels, lat_rows, rels):
@@ -316,6 +308,7 @@
             pltpu.VMEM((tokens, tiles * 128), F32),
             pltpu.VMEM((tiles, cell * slots, 128), F32),
             pltpu.VMEM((tokens, rows), BF16),
+            pltpu.VMEM((2 * pairs, slots, feat), BF16),
         ],
         compiler_params=pltpu.CompilerParams(vmem_limit_bytes=BLOCK_MB * 2**20),
         name="window_block",

time: 95.7 us -> 92.3 us (0.964)
  Pallas kernels: 21.2 us -> 18.3 us
    pallas_call x1, Pallas kernels: 12.5 us -> 10.6 us  [run_block(): pl.pallas_call(functools.partial(block_kernel, heads=heads, windows=windo...]
where the time goes in v2:
time: 92.3 us; the launch traced here: 91.8 us
  starting transfers between devices  34.5 us (37%)
  waiting for transfers between devices  26 us (28%)
  Pallas kernels  18.3 us (20%)
  local copies, waits for them, and re-layouts  6.99 us (8%)
  other arithmetic  5.13 us (6%)
    all_to_all x2, starting transfers between devices, spread_over_lat(): return lax.all_to_all(x, 'lat', 0, 0)  15.7 us
    all_to_all x2, waiting for transfers between devices, spread_over_lat(): return lax.all_to_all(x, 'lat', 0, 0)  15.1 us
    all_to_all x2, starting transfers between devices, spread_over_lon(): return lax.all_to_all(x, 'lon', 0, 0, axis_index_groups=groups)  11.7 us
    pallas_call x1, Pallas kernels, run_block(): pl.pallas_call(functools.partial(block_kernel, heads=heads, windows=windo...  10.6 us
    all_to_all x2, waiting for transfers between devices, spread_over_lon(): return lax.all_to_all(x, 'lon', 0, 0, axis_index_groups=groups)  8.95 us
    unnamed x15, local copies, waits for them, and re-layouts  4.95 us
    pallas_call x1, Pallas kernels, make_bias(): pl.pallas_call(functools.partial(bias_kernel, levels=levels, lat_rows=lat...  3.99 us
    ppermute x2, starting transfers between devices, shift(): lax.ppermute(x, 'lat', [(i, (i + lat_by) % lats) for i in range(lats)])  3.84 us
  transfers between devices with their start and end apart: 12, of which 4 were waited for; matrix products, arithmetic and copies ran while one was open for 8% of the time, Pallas kernels for 7%

profile of v2, /device:TPU:8, one launch (start us, length us, event | category | flops | bytes accessed | tf_op | source)
XLA Modules:
  0.0 91.8 jit_solution(33325545775408735)
XLA Ops:
  0.6 0.8 pad_maximum_fusion
  1.5 0.7 broadcast_in_dim.12
  2.1 11.0 %all-to-all-start = ((bf16[16,24,96]{2,1,0:T(8,128)(2,1)}), bf16[16,24,96]{2,1,0:T(8,128)(2,1)S(1)}, u32[]{:S(2)}, u32[]{:S(2)}) async-start(bf16[16,24,96]{2,1,0:T(8,128)(2,1)} %broadcast_in_dim.12), calls=%async_computation | async-start | bytes 196608 | tf_op jit(solution)/shard_map/all_to_all | solution.py:440
  13.2 1.0 %copy.32 = f32[1,12,6336]{2,1,0:T(8,128)S(1)} copy(f32[1,12,6336]{2,0,1:T(1,128)} %param.16) | data formatting | bytes 608256
  14.2 2.1 %maximum_bitcast_fusion = bf16[18,2,2,12,384]{4,2,0,3,1:T(2,128)(2,1)S(1)} fusion(bf16[1,2,12,18,384]{4,1,3,2,0:T(2,128)(2,1)} %bitcast.26, bf16[1,2,12,18,384]{4,1,3,2,0:T(2,128)(2,1)} %bitcast.27), kind=kLoop, calls=%fused_computation.3 | loop fusion | flops 331776 | bytes 1327104 | tf_op jit(solution)/shard_map/transpose | solution.py:463
  16.2 7.0 %all-to-all-done.x_ref = bf16[16,24,96]{2,1,0:T(8,128)(2,1)S(1)} async-done(((bf16[16,24,96]{2,1,0:T(8,128)(2,1)}), bf16[16,24,96]{2,1,0:T(8,128)(2,1)S(1)}, u32[]{:S(2)}, u32[]{:S(2)}) %all-to-all-start) | async-done | bytes 73760 | tf_op jit(solution)/shard_map/all_to_all | solution.py:440
  23.2 0.9 %turn_weights.1 = bf16[8,96,384]{2,1,0:T(8,128)(2,1)} custom-call(bf16[16,24,96]{2,1,0:T(8,128)(2,1)S(1)} %all-to-all-done.x_ref), custom_call_target="tpu_custom_call" | custom-call | tf_op jit(solution)/shard_map/turn_weights/pallas_call | solution.py:115
  24.2 5.1 %all-to-all-start.1 = ((bf16[8,96,384]{2,1,0:T(8,128)(2,1)}), bf16[8,96,384]{2,1,0:T(8,128)(2,1)S(1)}, u32[]{:S(2)}, u32[]{:S(2)}) async-start(bf16[8,96,384]{2,1,0:T(8,128)(2,1)} %turn_weights.1), calls=%async_computation.1 | async-start | bytes 1179648 | tf_op jit(solution)/shard_map/all_to_all | solution.py:446
  29.2 0.4 fusion.3
  29.6 2.2 %collective-permute-start = (bf16[15,2,2,6,384]{4,2,0,3,1:T(2,128)(2,1)S(1)}, bf16[15,2,2,6,384]{4,2,0,3,1:T(2,128)(2,1)S(1)}, u32[]{:S(2)}, u32[]{:S(2)}) collective-permute-start(bf16[15,2,2,6,384]{4,2,0,3,1:T(2,128)(2,1)S(1)} %get-tuple-element.83), channel_id=1, source_target_pairs={{0,240},{16,0},{32,16},{48,32},{64,48},{80,64},{96,80},{112,96},{1... | collective-permute-start | bytes 829448 | tf_op jit(solution)/shard_map/ppermute | solution.py:428
  32.0 0.3 collective-permute-start.1
  32.3 4.0 %make_bias.1.bias_ref = f32[12,144,144]{2,1,0:T(8,128)S(1)} custom-call(s32[1]{0:T(128)} %bitcast.1.last_ref, f32[12,6336]{1,0:T(8,128)S(1)} %bitcast.24, bf16[512,384]{1,0:T(8,128)(2,1)S(1)} %copy-done.1), custom_call_target="tpu_custom_call" | custom-call | tf_op jit(solution)/shard_map/make_bias/pallas_call | solution.py:90
  36.3 1.2 %copy-done = f32[12,144,144]{2,1,0:T(8,128)} copy-done((f32[12,144,144]{2,1,0:T(8,128)}, f32[12,144,144]{2,1,0:T(8,128)S(1)}, u32[]{:S(2)}) %copy-start) | copy-done | bytes 995352
  37.6 0.8 collective-permute-start.3
  38.4 1.0 %maximum_maximum_fusion = bf16[18,2,2,12,384]{4,2,0,3,1:T(2,128)(2,1)S(1)} fusion(bf16[3,2,2,6,384]{4,2,0,3,1:T(2,128)(2,1)S(1)} %collective-permute-done.2, bf16[3,2,2,6,384]{4,2,0,3,1:T(2,128)(2,1)S(1)} %collective-permute-done.1, bf16[15,2,2,6,384]{4,2,0,3,1:T(2,128)(2,1)S(1)} %collective-permute-done, bf16[15,2,2,6,384]{4,2,0,3,1:T(2,128)(2,1)S(1)} %get-tuple-element.38), kind=kLoop, calls=%fused_computation.4 | loop fusion | flops 995328 | bytes 1327104 | tf_op jit(solution)/shard_map/concatenate | solution.py:481
  39.4 0.5 fusion.1
  40.2 10.6 %window_block.1 = (bf16[8,112,384]{2,1,0:T(8,128)(2,1)S(1)}, bf16[8,112,384]{2,1,0:T(8,128)(2,1)S(1)}, bf16[12,32,432]{2,1,0:T(8,128)(2,1)S(1)}, bf16[12,96,144]...) custom-call(s32[1]{0:T(128)} %bitcast.me_ref, bf16[432,384]{1,0:T(8,128)(2,1)S(1)} %reshape_squeeze.6.x_ref, ...), custom_call_target="tpu_custom_call" | custom-call | tf_op jit(solution)/shard_map/window_block/pallas_call | solution.py:294
  50.8 0.3 collective-permute-start.4
  51.1 1.9 %collective-permute-done.4 = bf16[8,112,384]{2,1,0:T(8,128)(2,1)S(1)} collective-permute-done((bf16[8,112,384]{2,1,0:T(8,128)(2,1)S(1)}, bf16[8,112,384]{2,1,0:T(8,128)(2,1)S(1)}, u32[]{:S(2)}, u32[]{:S(2)}) %collective-permute-start.4) | collective-permute-done | bytes 688160 | tf_op jit(solution)/shard_map/ppermute | solution.py:422
  53.0 1.1 %add_convert_fusion = bf16[8,112,384]{2,1,0:T(8,128)(2,1)} fusion(bf16[8,112,384]{2,1,0:T(8,128)(2,1)S(1)} %collective-permute-done.4, bf16[8,112,384]{2,1,0:T(8,128)(2,1)S(1)} %get-tuple-element.44), kind=kLoop, calls=%fused_computation | loop fusion | flops 1376256 | bytes 2064384 | tf_op jit(solution)/shard_map/convert_element_type | solution.py:493
  54.1 6.6 %all-to-all-start.2 = ((bf16[8,112,384]{2,1,0:T(8,128)(2,1)}), bf16[8,112,384]{2,1,0:T(8,128)(2,1)S(1)}, u32[]{:S(2)}, u32[]{:S(2)}) async-start(bf16[8,112,384]{2,1,0:T(8,128)(2,1)} %add_convert_fusion), calls=%async_computation.2 | async-start | bytes 1376256 | tf_op jit(solution)/shard_map/all_to_all | solution.py:446
  60.7 1.1 %copy-done.3 = bf16[12,96,144]{2,1,0:T(8,128)(2,1)S(1)} copy-done((bf16[12,96,144]{2,1,0:T(8,128)(2,1)S(1)}, bf16[12,96,144]{2,1,0:T(8,128)(2,1)}, u32[]{:S(2)}) %copy-start.3) | copy-done | bytes 331800
  61.7 1.2 %input_gradient.1 = bf16[432,384]{1,0:T(8,128)(2,1)S(1)} custom-call(s32[1]{0:T(128)} %bitcast.me_ref, bf16[432,384]{1,0:T(8,128)(2,1)S(1)} %reshape_squeeze.6.x_ref, f32[1,384]{1,0:T(1,128)S(1)} %broadcast_in_dim.13.gain_ref, bf16[8,96,384]{2,1,0:T(8,128)(2,1)S(1)} %all-to-all-done.1.w_same_ref, bf16[8,96,384]{2,1,0:T(8,128)(2,1)S(1)} %collective-permute-done.3.w_other_ref, ...), custom_call_target="tpu_custom_call" | custom-call | tf_op jit(solution)/shard_map/input_gradient/pallas_call | solution.py:343
  63.1 1.7 %collective-permute-start.6 = (bf16[15,2,6,384]{3,2,1,0:T(8,128)(2,1)S(1)}, bf16[15,2,6,384]{3,2,1,0:T(8,128)(2,1)S(1)}, u32[]{:S(2)}, u32[]{:S(2)}) collective-permute-start(bf16[15,2,6,384]{3,2,1,0:T(8,128)(2,1)S(1)} %slice.59), channel_id=1, source_target_pairs={{0,16},{16,32},{32,48},{48,64},{64,80},{80,96},{96,112},{112,128},... | collective-permute-start | bytes 414728 | tf_op jit(solution)/shard_map/ppermute | solution.py:428
  64.9 1.6 %collective-permute-start.5 = (bf16[3,2,6,384]{3,2,1,0:T(8,128)(2,1)S(1)}, bf16[3,2,6,384]{3,2,1,0:T(8,128)(2,1)S(1)}, u32[]{:S(2)}, u32[]{:S(2)}) collective-permute-start(bf16[3,2,6,384]{3,2,1,0:T(8,128)(2,1)S(1)} %get-tuple-element.86), channel_id=1, source_target_pairs={{0,1},{1,2},{2,3},{3,4},{4,5},{5,6},{6,7},{7,8},{8,9},{9,10},{10,1... | collective-permute-start | bytes 82952 | tf_op jit(solution)/shard_map/ppermute | solution.py:430
  66.4 8.9 %all-to-all-done.2.x_ref = bf16[8,112,384]{2,1,0:T(8,128)(2,1)S(1)} async-done(((bf16[8,112,384]{2,1,0:T(8,128)(2,1)}), bf16[8,112,384]{2,1,0:T(8,128)(2,1)S(1)}, u32[]{:S(2)}, u32[]{:S(2)}) %all-to-all-start.2) | async-done | bytes 688160 | tf_op jit(solution)/shard_map/all_to_all | solution.py:446
  75.4 0.9 sum_and_turn.1
  76.3 4.7 %all-to-all-start.3 = ((bf16[16,32,96]{2,1,0:T(8,128)(2,1)}), bf16[16,32,96]{2,1,0:T(8,128)(2,1)S(1)}, u32[]{:S(2)}, u32[]{:S(2)}) async-start(bf16[16,32,96]{2,1,0:T(8,128)(2,1)} %get-tuple-element.54), calls=%async_computation.3 | async-start | bytes 262144 | tf_op jit(solution)/shard_map/all_to_all | solution.py:440
  81.1 0.6 copy.28
  81.9 1.0 %copy.27 = bf16[2,12,18,384]{3,0,2,1:T(2,128)(2,1)} copy(bf16[2,12,18,384]{3,1,0,2:T(8,128)(2,1)S(1)} %fusion) | data formatting | bytes 663552
  82.9 8.2 %all-to-all-done.3.x_ref = bf16[16,32,96]{2,1,0:T(8,128)(2,1)S(1)} async-done(((bf16[16,32,96]{2,1,0:T(8,128)(2,1)}), bf16[16,32,96]{2,1,0:T(8,128)(2,1)S(1)}, u32[]{:S(2)}, u32[]{:S(2)}) %all-to-all-start.3) | async-done | bytes 98336 | tf_op jit(solution)/shard_map/all_to_all | solution.py:440
  91.1 0.7 last_sum.1
  (35 shorter events, 1.0 us)
Async XLA Ops:
  2.1 21.1 %all-to-all-start = ((bf16[16,24,96]{2,1,0:T(8,128)(2,1)}), bf16[16,24,96]{2,1,0:T(8,128)(2,1)S(1)}, u32[]{:S(2)}, u32[]{:S(2)}) async-start(bf16[16,24,96]{2,1,0:T(8,128)(2,1)} %broadcast_in_dim.12), calls=%async_computation | async-start | bytes 196608 | tf_op jit(solution)/shard_map/all_to_all | solution.py:440
  24.2 8.1 %copy-start.1 = (bf16[512,384]{1,0:T(8,128)(2,1)S(1)}, bf16[512,384]{1,0:T(8,128)(2,1)}, u32[]{:S(2)}) copy-start(bf16[512,384]{1,0:T(8,128)(2,1)} %constant.11.clone.order_ref) | copy-start | bytes 1179652
  24.2 13.4 %all-to-all-start.1 = ((bf16[8,96,384]{2,1,0:T(8,128)(2,1)}), bf16[8,96,384]{2,1,0:T(8,128)(2,1)S(1)}, u32[]{:S(2)}, u32[]{:S(2)}) async-start(bf16[8,96,384]{2,1,0:T(8,128)(2,1)} %turn_weights.1), calls=%async_computation.1 | async-start | bytes 1179648 | tf_op jit(solution)/shard_map/all_to_all | solution.py:446
  29.6 8.8 %copy-start.5 = (f32[384]{0:T(512)S(1)}, f32[384]{0:T(512)}, u32[]{:S(2)}) copy-start(f32[384]{0:T(512)} %param.11) | copy-start | bytes 4612
  29.6 7.9 %collective-permute-start = (bf16[15,2,2,6,384]{4,2,0,3,1:T(2,128)(2,1)S(1)}, bf16[15,2,2,6,384]{4,2,0,3,1:T(2,128)(2,1)S(1)}, u32[]{:S(2)}, u32[]{:S(2)}) collective-permute-start(bf16[15,2,2,6,384]{4,2,0,3,1:T(2,128)(2,1)S(1)} %get-tuple-element.83), channel_id=1, source_target_pairs={{0,240},{16,0},{32,16},{48,32},{64,48},{80,64},{96,80},{112,96},{1... | collective-permute-start | bytes 829448 | tf_op jit(solution)/shard_map/ppermute | solution.py:428
  31.9 5.7 %collective-permute-start.2 = (bf16[3,2,2,6,384]{4,2,0,3,1:T(2,128)(2,1)S(1)}, bf16[3,2,2,6,384]{4,2,0,3,1:T(2,128)(2,1)S(1)}, u32[]{:S(2)}, u32[]{:S(2)}) collective-permute-start(bf16[3,2,2,6,384]{4,2,0,3,1:T(2,128)(2,1)S(1)} %get-tuple-element.81), channel_id=1, source_target_pairs={{0,255},{1,240},{2,241},{3,242},{4,243},{5,244},{6,245},{7,246},{8... | collective-permute-start | bytes 165896 | tf_op jit(solution)/shard_map/ppermute | solution.py:436
  32.0 5.6 %collective-permute-start.1 = (bf16[3,2,2,6,384]{4,2,0,3,1:T(2,128)(2,1)S(1)}, bf16[3,2,2,6,384]{4,2,0,3,1:T(2,128)(2,1)S(1)}, u32[]{:S(2)}, u32[]{:S(2)}) collective-permute-start(bf16[3,2,2,6,384]{4,2,0,3,1:T(2,128)(2,1)S(1)} %get-tuple-element.82), channel_id=1, source_target_pairs={{0,15},{1,0},{2,1},{3,2},{4,3},{5,4},{6,5},{7,6},{8,7},{9,8},{10,9... | collective-permute-start | bytes 165896 | tf_op jit(solution)/shard_map/ppermute | solution.py:430
  36.3 1.3 %copy-start = (f32[12,144,144]{2,1,0:T(8,128)}, f32[12,144,144]{2,1,0:T(8,128)S(1)}, u32[]{:S(2)}) copy-start(f32[12,144,144]{2,1,0:T(8,128)S(1)} %make_bias.1.bias_ref) | copy-start | bytes 2985988
  37.6 2.6 %collective-permute-start.3 = (bf16[8,96,384]{2,1,0:T(8,128)(2,1)S(1)}, bf16[8,96,384]{2,1,0:T(8,128)(2,1)S(1)}, u32[]{:S(2)}, u32[]{:S(2)}) collective-permute-start(bf16[8,96,384]{2,1,0:T(8,128)(2,1)S(1)} %all-to-all-done.1.w_same_ref), channel_id=1, source_target_pairs={{0,1},{1,0},{2,3},{3,2},{4,5},{5,4},{6,7},{7,6},{8,9},{9,8},{10,11... | collective-permute-start | bytes 1769480 | tf_op jit(solution)/shard_map/ppermute | solution.py:422
  50.8 3.3 %copy-start.2 = (bf16[12,96,144]{2,1,0:T(8,128)(2,1)}, bf16[12,96,144]{2,1,0:T(8,128)(2,1)S(1)}, u32[]{:S(2)}) copy-start(bf16[12,96,144]{2,1,0:T(8,128)(2,1)S(1)} %get-tuple-element.51.dv_ref) | copy-start | bytes 995332
  50.8 2.2 %collective-permute-start.4 = (bf16[8,112,384]{2,1,0:T(8,128)(2,1)S(1)}, bf16[8,112,384]{2,1,0:T(8,128)(2,1)S(1)}, u32[]{:S(2)}, u32[]{:S(2)}) collective-permute-start(bf16[8,112,384]{2,1,0:T(8,128)(2,1)S(1)} %get-tuple-element.45), channel_id=1, source_target_pairs={{0,1},{1,0},{2,3},{3,2},{4,5},{5,4},{6,7},{7,6},{8,9},{9,8},{10,11... | collective-permute-start | bytes 2064392 | tf_op jit(solution)/shard_map/ppermute | solution.py:422
  54.1 21.3 %all-to-all-start.2 = ((bf16[8,112,384]{2,1,0:T(8,128)(2,1)}), bf16[8,112,384]{2,1,0:T(8,128)(2,1)S(1)}, u32[]{:S(2)}, u32[]{:S(2)}) async-start(bf16[8,112,384]{2,1,0:T(8,128)(2,1)} %add_convert_fusion), calls=%async_computation.2 | async-start | bytes 1376256 | tf_op jit(solution)/shard_map/all_to_all | solution.py:446
  60.7 1.1 %copy-start.3 = (bf16[12,96,144]{2,1,0:T(8,128)(2,1)S(1)}, bf16[12,96,144]{2,1,0:T(8,128)(2,1)}, u32[]{:S(2)}) copy-start(bf16[12,96,144]{2,1,0:T(8,128)(2,1)} %copy-done.2) | copy-start | bytes 995332
  62.9 18.8 %copy-start.4 = (bf16[2,12,18,384]{3,0,2,1:T(2,128)(2,1)S(1)}, bf16[2,12,18,384]{3,0,2,1:T(2,128)(2,1)}, u32[]{:S(2)}) copy-start(bf16[2,12,18,384]{3,0,2,1:T(2,128)(2,1)} %param.10) | copy-start | bytes 995332
  63.1 17.9 %collective-permute-start.6 = (bf16[15,2,6,384]{3,2,1,0:T(8,128)(2,1)S(1)}, bf16[15,2,6,384]{3,2,1,0:T(8,128)(2,1)S(1)}, u32[]{:S(2)}, u32[]{:S(2)}) collective-permute-start(bf16[15,2,6,384]{3,2,1,0:T(8,128)(2,1)S(1)} %slice.59), channel_id=1, source_target_pairs={{0,16},{16,32},{32,48},{48,64},{64,80},{80,96},{96,112},{112,128},... | collective-permute-start | bytes 414728 | tf_op jit(solution)/shard_map/ppermute | solution.py:428
  64.8 16.2 %collective-permute-start.7 = (bf16[3,2,6,384]{3,2,1,0:T(8,128)(2,1)S(1)}, bf16[3,2,6,384]{3,2,1,0:T(8,128)(2,1)S(1)}, u32[]{:S(2)}, u32[]{:S(2)}) collective-permute-start(bf16[3,2,6,384]{3,2,1,0:T(8,128)(2,1)S(1)} %get-tuple-element.85), channel_id=1, source_target_pairs={{0,17},{1,18},{2,19},{3,20},{4,21},{5,22},{6,23},{7,24},{8,25},{9,... | collective-permute-start | bytes 82952 | tf_op jit(solution)/shard_map/ppermute | solution.py:436
  64.9 16.1 %collective-permute-start.5 = (bf16[3,2,6,384]{3,2,1,0:T(8,128)(2,1)S(1)}, bf16[3,2,6,384]{3,2,1,0:T(8,128)(2,1)S(1)}, u32[]{:S(2)}, u32[]{:S(2)}) collective-permute-start(bf16[3,2,6,384]{3,2,1,0:T(8,128)(2,1)S(1)} %get-tuple-element.86), channel_id=1, source_target_pairs={{0,1},{1,2},{2,3},{3,4},{4,5},{5,6},{6,7},{7,8},{8,9},{9,10},{10,1... | collective-permute-start | bytes 82952 | tf_op jit(solution)/shard_map/ppermute | solution.py:430
  76.3 14.8 %all-to-all-start.3 = ((bf16[16,32,96]{2,1,0:T(8,128)(2,1)}), bf16[16,32,96]{2,1,0:T(8,128)(2,1)S(1)}, u32[]{:S(2)}, u32[]{:S(2)}) async-start(bf16[16,32,96]{2,1,0:T(8,128)(2,1)} %get-tuple-element.54), calls=%async_computation.3 | async-start | bytes 262144 | tf_op jit(solution)/shard_map/all_to_all | solution.py:440

commit v3 on v2

--- a/solution.py
+++ b/solution.py
@@ -12,7 +12,6 @@
 EPSILON = 1e-05
 MASKED = -1000000000.0
 LOG2E = math.log2(math.e)
-UNROLL = 12
 BLOCK_MB = 48
 SMALL_MB = 16
 F32 = jnp.float32
@@ -67,7 +66,7 @@
     crossing = (row_north != lane_north) & (last_ref[0] != 0)
     strips = jnp.where(crossing, MASKED, strips) * LOG2E
     for g in range(tiles):
-        strips_s[g] = strips[:, g * 128:(g + 1) * 128]
+        strips_s[g, 0:cell * slots, :] = strips[:, g * 128:(g + 1) * 128]
 
     def head(h, carry):
         strip = jnp.concatenate([strips_s[g, pl.ds(h, cell, stride=slots), :] for g in range(tiles)], axis=1)
@@ -94,7 +93,7 @@
         out_specs=vmem,
         scratch_shapes=[
             pltpu.VMEM((cell, slots, order.shape[0]), F32),
-            pltpu.VMEM((tiles, cell * slots, 128), F32),
+            pltpu.VMEM((tiles, (cell + 1) * slots, 128), F32),
             pltpu.VMEM((tokens, tokens), F32),
         ],
         compiler_params=pltpu.CompilerParams(vmem_limit_bytes=SMALL_MB * 2**20),
@@ -156,7 +155,7 @@
     scale = 1.0 / math.sqrt(dim)
     tiles = fold_s.shape[0]
     lanes = tiles * 128
-    slots = fold_s.shape[1] // cell
+    slots = fold_s.shape[1] // (cell + 1)
     pairs, packed, _ = w_same_ref.shape
     part = packed // 4
     parity = me_ref[0] % 2
@@ -220,8 +219,7 @@
             fold_s[g, pl.ds(h, cell, stride=slots), :] = folded[:, g * 128:(g + 1) * 128]
         return carry
 
-    if UNROLL:
-        lax.fori_loop(0, heads, head, 0, unroll=UNROLL)
+    lax.fori_loop(0, heads, head, 0, unroll=True)
 
     def by_window(ref, w):
         return ref[:, w * dim:(w + 1) * dim, :].reshape(feat, tokens)
@@ -238,7 +236,7 @@
         g_gain = g_gain + jnp.sum(gw_s[i] * w_s[i], axis=0, keepdims=True)
     g_gain = g_gain / gain_ref[...]
 
-    fold = jnp.concatenate([fold_s[g] for g in range(tiles)], axis=1).astype(BF16)
+    fold = jnp.concatenate([fold_s[g, 0:cell * slots, :] for g in range(tiles)], axis=1).astype(BF16)
     back = mm(fold, order_ref[...], NT)
     width = lat_rows * rels
     half = back.shape[1] // levels
@@ -306,7 +304,7 @@
             pltpu.VMEM((heads, windows * dim, tokens), BF16),
             pltpu.VMEM((heads, dim, rows), BF16),
             pltpu.VMEM((tokens, tiles * 128), F32),
-            pltpu.VMEM((tiles, cell * slots, 128), F32),
+            pltpu.VMEM((tiles, (cell + 1) * slots, 128), F32),
             pltpu.VMEM((tokens, rows), BF16),
             pltpu.VMEM((2 * pairs, slots, feat), BF16),
         ],

time: 92.3 us -> 92.3 us (level)
  no operation moved by 1% of the time
where the time goes in v3:
time: 92.3 us; the launch traced here: 91.7 us
  starting transfers between devices  34.5 us (37%)
  waiting for transfers between devices  26 us (28%)
  Pallas kernels  18.2 us (20%)
  local copies, waits for them, and re-layouts  6.99 us (8%)
  other arithmetic  5.13 us (6%)
    all_to_all x2, starting transfers between devices, spread_over_lat(): return lax.all_to_all(x, 'lat', 0, 0)  15.7 us
    all_to_all x2, waiting for transfers between devices, spread_over_lat(): return lax.all_to_all(x, 'lat', 0, 0)  15.1 us
    all_to_all x2, starting transfers between devices, spread_over_lon(): return lax.all_to_all(x, 'lon', 0, 0, axis_index_groups=groups)  11.7 us
    pallas_call x1, Pallas kernels, run_block(): pl.pallas_call(functools.partial(block_kernel, heads=heads, windows=windo...  10.5 us
    all_to_all x2, waiting for transfers between devices, spread_over_lon(): return lax.all_to_all(x, 'lon', 0, 0, axis_index_groups=groups)  8.94 us
    unnamed x15, local copies, waits for them, and re-layouts  4.95 us
    pallas_call x1, Pallas kernels, make_bias(): pl.pallas_call(functools.partial(bias_kernel, levels=levels, lat_rows=lat...  3.98 us
    ppermute x2, starting transfers between devices, shift(): lax.ppermute(x, 'lat', [(i, (i + lat_by) % lats) for i in range(lats)])  3.84 us
  transfers between devices with their start and end apart: 12, of which 4 were waited for; matrix products, arithmetic and copies ran while one was open for 8% of the time, Pallas kernels for 7%

profile of v3, /device:TPU:8, one launch (start us, length us, event | category | flops | bytes accessed | tf_op | source)
XLA Modules:
  0.0 91.7 jit_solution(4818685135378828648)
XLA Ops:
  0.6 0.8 pad_maximum_fusion
  1.5 0.7 broadcast_in_dim.12
  2.1 11.0 %all-to-all-start = ((bf16[16,24,96]{2,1,0:T(8,128)(2,1)}), bf16[16,24,96]{2,1,0:T(8,128)(2,1)S(1)}, u32[]{:S(2)}, u32[]{:S(2)}) async-start(bf16[16,24,96]{2,1,0:T(8,128)(2,1)} %broadcast_in_dim.12), calls=%async_computation | async-start | bytes 196608 | tf_op jit(solution)/shard_map/all_to_all | solution.py:438
  13.2 1.0 %copy.32 = f32[1,12,6336]{2,1,0:T(8,128)S(1)} copy(f32[1,12,6336]{2,0,1:T(1,128)} %param.16) | data formatting | bytes 608256
  14.2 2.1 %maximum_bitcast_fusion = bf16[18,2,2,12,384]{4,2,0,3,1:T(2,128)(2,1)S(1)} fusion(bf16[1,2,12,18,384]{4,1,3,2,0:T(2,128)(2,1)} %bitcast.26, bf16[1,2,12,18,384]{4,1,3,2,0:T(2,128)(2,1)} %bitcast.27), kind=kLoop, calls=%fused_computation.3 | loop fusion | flops 331776 | bytes 1327104 | tf_op jit(solution)/shard_map/transpose | solution.py:461
  16.2 7.0 %all-to-all-done.x_ref = bf16[16,24,96]{2,1,0:T(8,128)(2,1)S(1)} async-done(((bf16[16,24,96]{2,1,0:T(8,128)(2,1)}), bf16[16,24,96]{2,1,0:T(8,128)(2,1)S(1)}, u32[]{:S(2)}, u32[]{:S(2)}) %all-to-all-start) | async-done | bytes 73760 | tf_op jit(solution)/shard_map/all_to_all | solution.py:438
  23.2 0.9 %turn_weights.1 = bf16[8,96,384]{2,1,0:T(8,128)(2,1)} custom-call(bf16[16,24,96]{2,1,0:T(8,128)(2,1)S(1)} %all-to-all-done.x_ref), custom_call_target="tpu_custom_call" | custom-call | tf_op jit(solution)/shard_map/turn_weights/pallas_call | solution.py:114
  24.2 5.1 %all-to-all-start.1 = ((bf16[8,96,384]{2,1,0:T(8,128)(2,1)}), bf16[8,96,384]{2,1,0:T(8,128)(2,1)S(1)}, u32[]{:S(2)}, u32[]{:S(2)}) async-start(bf16[8,96,384]{2,1,0:T(8,128)(2,1)} %turn_weights.1), calls=%async_computation.1 | async-start | bytes 1179648 | tf_op jit(solution)/shard_map/all_to_all | solution.py:444
  29.2 0.4 fusion.3
  29.6 2.2 %collective-permute-start = (bf16[15,2,2,6,384]{4,2,0,3,1:T(2,128)(2,1)S(1)}, bf16[15,2,2,6,384]{4,2,0,3,1:T(2,128)(2,1)S(1)}, u32[]{:S(2)}, u32[]{:S(2)}) collective-permute-start(bf16[15,2,2,6,384]{4,2,0,3,1:T(2,128)(2,1)S(1)} %get-tuple-element.83), channel_id=1, source_target_pairs={{0,240},{16,0},{32,16},{48,32},{64,48},{80,64},{96,80},{112,96},{1... | collective-permute-start | bytes 829448 | tf_op jit(solution)/shard_map/ppermute | solution.py:426
  32.0 0.3 collective-permute-start.1
  32.3 4.0 %make_bias.1.bias_ref = f32[12,144,144]{2,1,0:T(8,128)S(1)} custom-call(s32[1]{0:T(128)} %bitcast.1.last_ref, f32[12,6336]{1,0:T(8,128)S(1)} %bitcast.24, bf16[512,384]{1,0:T(8,128)(2,1)S(1)} %copy-done.1), custom_call_target="tpu_custom_call" | custom-call | tf_op jit(solution)/shard_map/make_bias/pallas_call | solution.py:89
  36.3 1.2 %copy-done = f32[12,144,144]{2,1,0:T(8,128)} copy-done((f32[12,144,144]{2,1,0:T(8,128)}, f32[12,144,144]{2,1,0:T(8,128)S(1)}, u32[]{:S(2)}) %copy-start) | copy-done | bytes 995352
  37.6 0.9 collective-permute-start.3
  38.4 1.0 %maximum_maximum_fusion = bf16[18,2,2,12,384]{4,2,0,3,1:T(2,128)(2,1)S(1)} fusion(bf16[3,2,2,6,384]{4,2,0,3,1:T(2,128)(2,1)S(1)} %collective-permute-done.2, bf16[3,2,2,6,384]{4,2,0,3,1:T(2,128)(2,1)S(1)} %collective-permute-done.1, bf16[15,2,2,6,384]{4,2,0,3,1:T(2,128)(2,1)S(1)} %collective-permute-done, bf16[15,2,2,6,384]{4,2,0,3,1:T(2,128)(2,1)S(1)} %get-tuple-element.38), kind=kLoop, calls=%fused_computation.4 | loop fusion | flops 995328 | bytes 1327104 | tf_op jit(solution)/shard_map/concatenate | solution.py:479
  39.4 0.5 fusion.1
  40.2 10.5 %window_block.1 = (bf16[8,112,384]{2,1,0:T(8,128)(2,1)S(1)}, bf16[8,112,384]{2,1,0:T(8,128)(2,1)S(1)}, bf16[12,32,432]{2,1,0:T(8,128)(2,1)S(1)}, bf16[12,96,144]...) custom-call(s32[1]{0:T(128)} %bitcast.me_ref, bf16[432,384]{1,0:T(8,128)(2,1)S(1)} %reshape_squeeze.6.x_ref, ...), custom_call_target="tpu_custom_call" | custom-call | tf_op jit(solution)/shard_map/window_block/pallas_call | solution.py:292
  50.7 0.3 collective-permute-start.4
  51.0 1.9 %collective-permute-done.4 = bf16[8,112,384]{2,1,0:T(8,128)(2,1)S(1)} collective-permute-done((bf16[8,112,384]{2,1,0:T(8,128)(2,1)S(1)}, bf16[8,112,384]{2,1,0:T(8,128)(2,1)S(1)}, u32[]{:S(2)}, u32[]{:S(2)}) %collective-permute-start.4) | collective-permute-done | bytes 688160 | tf_op jit(solution)/shard_map/ppermute | solution.py:420
  53.0 1.1 %add_convert_fusion = bf16[8,112,384]{2,1,0:T(8,128)(2,1)} fusion(bf16[8,112,384]{2,1,0:T(8,128)(2,1)S(1)} %collective-permute-done.4, bf16[8,112,384]{2,1,0:T(8,128)(2,1)S(1)} %get-tuple-element.44), kind=kLoop, calls=%fused_computation | loop fusion | flops 1376256 | bytes 2064384 | tf_op jit(solution)/shard_map/convert_element_type | solution.py:491
  54.0 6.6 %all-to-all-start.2 = ((bf16[8,112,384]{2,1,0:T(8,128)(2,1)}), bf16[8,112,384]{2,1,0:T(8,128)(2,1)S(1)}, u32[]{:S(2)}, u32[]{:S(2)}) async-start(bf16[8,112,384]{2,1,0:T(8,128)(2,1)} %add_convert_fusion), calls=%async_computation.2 | async-start | bytes 1376256 | tf_op jit(solution)/shard_map/all_to_all | solution.py:444
  60.6 1.1 %copy-done.3 = bf16[12,96,144]{2,1,0:T(8,128)(2,1)S(1)} copy-done((bf16[12,96,144]{2,1,0:T(8,128)(2,1)S(1)}, bf16[12,96,144]{2,1,0:T(8,128)(2,1)}, u32[]{:S(2)}) %copy-start.3) | copy-done | bytes 331800
  61.7 1.2 %input_gradient.1 = bf16[432,384]{1,0:T(8,128)(2,1)S(1)} custom-call(s32[1]{0:T(128)} %bitcast.me_ref, bf16[432,384]{1,0:T(8,128)(2,1)S(1)} %reshape_squeeze.6.x_ref, f32[1,384]{1,0:T(1,128)S(1)} %broadcast_in_dim.13.gain_ref, bf16[8,96,384]{2,1,0:T(8,128)(2,1)S(1)} %all-to-all-done.1.w_same_ref, bf16[8,96,384]{2,1,0:T(8,128)(2,1)S(1)} %collective-permute-done.3.w_other_ref, ...), custom_call_target="tpu_custom_call" | custom-call | tf_op jit(solution)/shard_map/input_gradient/pallas_call | solution.py:341
  63.0 1.7 %collective-permute-start.6 = (bf16[15,2,6,384]{3,2,1,0:T(8,128)(2,1)S(1)}, bf16[15,2,6,384]{3,2,1,0:T(8,128)(2,1)S(1)}, u32[]{:S(2)}, u32[]{:S(2)}) collective-permute-start(bf16[15,2,6,384]{3,2,1,0:T(8,128)(2,1)S(1)} %slice.59), channel_id=1, source_target_pairs={{0,16},{16,32},{32,48},{48,64},{64,80},{80,96},{96,112},{112,128},... | collective-permute-start | bytes 414728 | tf_op jit(solution)/shard_map/ppermute | solution.py:426
  64.8 1.6 %collective-permute-start.5 = (bf16[3,2,6,384]{3,2,1,0:T(8,128)(2,1)S(1)}, bf16[3,2,6,384]{3,2,1,0:T(8,128)(2,1)S(1)}, u32[]{:S(2)}, u32[]{:S(2)}) collective-permute-start(bf16[3,2,6,384]{3,2,1,0:T(8,128)(2,1)S(1)} %get-tuple-element.86), channel_id=1, source_target_pairs={{0,1},{1,2},{2,3},{3,4},{4,5},{5,6},{6,7},{7,8},{8,9},{9,10},{10,1... | collective-permute-start | bytes 82952 | tf_op jit(solution)/shard_map/ppermute | solution.py:428
  66.4 8.9 %all-to-all-done.2.x_ref = bf16[8,112,384]{2,1,0:T(8,128)(2,1)S(1)} async-done(((bf16[8,112,384]{2,1,0:T(8,128)(2,1)}), bf16[8,112,384]{2,1,0:T(8,128)(2,1)S(1)}, u32[]{:S(2)}, u32[]{:S(2)}) %all-to-all-start.2) | async-done | bytes 688160 | tf_op jit(solution)/shard_map/all_to_all | solution.py:444
  75.3 0.9 sum_and_turn.1
  76.2 4.7 %all-to-all-start.3 = ((bf16[16,32,96]{2,1,0:T(8,128)(2,1)}), bf16[16,32,96]{2,1,0:T(8,128)(2,1)S(1)}, u32[]{:S(2)}, u32[]{:S(2)}) async-start(bf16[16,32,96]{2,1,0:T(8,128)(2,1)} %get-tuple-element.54), calls=%async_computation.3 | async-start | bytes 262144 | tf_op jit(solution)/shard_map/all_to_all | solution.py:438
  81.0 0.6 copy.28
  81.9 1.0 %copy.27 = bf16[2,12,18,384]{3,0,2,1:T(2,128)(2,1)} copy(bf16[2,12,18,384]{3,1,0,2:T(8,128)(2,1)S(1)} %fusion) | data formatting | bytes 663552
  82.8 8.2 %all-to-all-done.3.x_ref = bf16[16,32,96]{2,1,0:T(8,128)(2,1)S(1)} async-done(((bf16[16,32,96]{2,1,0:T(8,128)(2,1)}), bf16[16,32,96]{2,1,0:T(8,128)(2,1)S(1)}, u32[]{:S(2)}, u32[]{:S(2)}) %all-to-all-start.3) | async-done | bytes 98336 | tf_op jit(solution)/shard_map/all_to_all | solution.py:438
  91.0 0.7 last_sum.1
  (35 shorter events, 1.0 us)
Async XLA Ops:
  2.1 21.1 %all-to-all-start = ((bf16[16,24,96]{2,1,0:T(8,128)(2,1)}), bf16[16,24,96]{2,1,0:T(8,128)(2,1)S(1)}, u32[]{:S(2)}, u32[]{:S(2)}) async-start(bf16[16,24,96]{2,1,0:T(8,128)(2,1)} %broadcast_in_dim.12), calls=%async_computation | async-start | bytes 196608 | tf_op jit(solution)/shard_map/all_to_all | solution.py:438
  24.2 8.1 %copy-start.1 = (bf16[512,384]{1,0:T(8,128)(2,1)S(1)}, bf16[512,384]{1,0:T(8,128)(2,1)}, u32[]{:S(2)}) copy-start(bf16[512,384]{1,0:T(8,128)(2,1)} %constant.11.clone.order_ref) | copy-start | bytes 1179652
  24.2 13.4 %all-to-all-start.1 = ((bf16[8,96,384]{2,1,0:T(8,128)(2,1)}), bf16[8,96,384]{2,1,0:T(8,128)(2,1)S(1)}, u32[]{:S(2)}, u32[]{:S(2)}) async-start(bf16[8,96,384]{2,1,0:T(8,128)(2,1)} %turn_weights.1), calls=%async_computation.1 | async-start | bytes 1179648 | tf_op jit(solution)/shard_map/all_to_all | solution.py:444
  29.6 8.8 %copy-start.5 = (f32[384]{0:T(512)S(1)}, f32[384]{0:T(512)}, u32[]{:S(2)}) copy-start(f32[384]{0:T(512)} %param.11) | copy-start | bytes 4612
  29.6 7.9 %collective-permute-start = (bf16[15,2,2,6,384]{4,2,0,3,1:T(2,128)(2,1)S(1)}, bf16[15,2,2,6,384]{4,2,0,3,1:T(2,128)(2,1)S(1)}, u32[]{:S(2)}, u32[]{:S(2)}) collective-permute-start(bf16[15,2,2,6,384]{4,2,0,3,1:T(2,128)(2,1)S(1)} %get-tuple-element.83), channel_id=1, source_target_pairs={{0,240},{16,0},{32,16},{48,32},{64,48},{80,64},{96,80},{112,96},{1... | collective-permute-start | bytes 829448 | tf_op jit(solution)/shard_map/ppermute | solution.py:426
  31.9 5.7 %collective-permute-start.2 = (bf16[3,2,2,6,384]{4,2,0,3,1:T(2,128)(2,1)S(1)}, bf16[3,2,2,6,384]{4,2,0,3,1:T(2,128)(2,1)S(1)}, u32[]{:S(2)}, u32[]{:S(2)}) collective-permute-start(bf16[3,2,2,6,384]{4,2,0,3,1:T(2,128)(2,1)S(1)} %get-tuple-element.81), channel_id=1, source_target_pairs={{0,255},{1,240},{2,241},{3,242},{4,243},{5,244},{6,245},{7,246},{8... | collective-permute-start | bytes 165896 | tf_op jit(solution)/shard_map/ppermute | solution.py:434
  32.0 5.6 %collective-permute-start.1 = (bf16[3,2,2,6,384]{4,2,0,3,1:T(2,128)(2,1)S(1)}, bf16[3,2,2,6,384]{4,2,0,3,1:T(2,128)(2,1)S(1)}, u32[]{:S(2)}, u32[]{:S(2)}) collective-permute-start(bf16[3,2,2,6,384]{4,2,0,3,1:T(2,128)(2,1)S(1)} %get-tuple-element.82), channel_id=1, source_target_pairs={{0,15},{1,0},{2,1},{3,2},{4,3},{5,4},{6,5},{7,6},{8,7},{9,8},{10,9... | collective-permute-start | bytes 165896 | tf_op jit(solution)/shard_map/ppermute | solution.py:428
  36.3 1.3 %copy-start = (f32[12,144,144]{2,1,0:T(8,128)}, f32[12,144,144]{2,1,0:T(8,128)S(1)}, u32[]{:S(2)}) copy-start(f32[12,144,144]{2,1,0:T(8,128)S(1)} %make_bias.1.bias_ref) | copy-start | bytes 2985988
  37.6 2.6 %collective-permute-start.3 = (bf16[8,96,384]{2,1,0:T(8,128)(2,1)S(1)}, bf16[8,96,384]{2,1,0:T(8,128)(2,1)S(1)}, u32[]{:S(2)}, u32[]{:S(2)}) collective-permute-start(bf16[8,96,384]{2,1,0:T(8,128)(2,1)S(1)} %all-to-all-done.1.w_same_ref), channel_id=1, source_target_pairs={{0,1},{1,0},{2,3},{3,2},{4,5},{5,4},{6,7},{7,6},{8,9},{9,8},{10,11... | collective-permute-start | bytes 1769480 | tf_op jit(solution)/shard_map/ppermute | solution.py:420
  50.7 3.3 %copy-start.2 = (bf16[12,96,144]{2,1,0:T(8,128)(2,1)}, bf16[12,96,144]{2,1,0:T(8,128)(2,1)S(1)}, u32[]{:S(2)}) copy-start(bf16[12,96,144]{2,1,0:T(8,128)(2,1)S(1)} %get-tuple-element.51.dv_ref) | copy-start | bytes 995332
  50.7 2.2 %collective-permute-start.4 = (bf16[8,112,384]{2,1,0:T(8,128)(2,1)S(1)}, bf16[8,112,384]{2,1,0:T(8,128)(2,1)S(1)}, u32[]{:S(2)}, u32[]{:S(2)}) collective-permute-start(bf16[8,112,384]{2,1,0:T(8,128)(2,1)S(1)} %get-tuple-element.45), channel_id=1, source_target_pairs={{0,1},{1,0},{2,3},{3,2},{4,5},{5,4},{6,7},{7,6},{8,9},{9,8},{10,11... | collective-permute-start | bytes 2064392 | tf_op jit(solution)/shard_map/ppermute | solution.py:420
  54.0 21.3 %all-to-all-start.2 = ((bf16[8,112,384]{2,1,0:T(8,128)(2,1)}), bf16[8,112,384]{2,1,0:T(8,128)(2,1)S(1)}, u32[]{:S(2)}, u32[]{:S(2)}) async-start(bf16[8,112,384]{2,1,0:T(8,128)(2,1)} %add_convert_fusion), calls=%async_computation.2 | async-start | bytes 1376256 | tf_op jit(solution)/shard_map/all_to_all | solution.py:444
  60.6 1.1 %copy-start.3 = (bf16[12,96,144]{2,1,0:T(8,128)(2,1)S(1)}, bf16[12,96,144]{2,1,0:T(8,128)(2,1)}, u32[]{:S(2)}) copy-start(bf16[12,96,144]{2,1,0:T(8,128)(2,1)} %copy-done.2) | copy-start | bytes 995332
  62.9 18.8 %copy-start.4 = (bf16[2,12,18,384]{3,0,2,1:T(2,128)(2,1)S(1)}, bf16[2,12,18,384]{3,0,2,1:T(2,128)(2,1)}, u32[]{:S(2)}) copy-start(bf16[2,12,18,384]{3,0,2,1:T(2,128)(2,1)} %param.10) | copy-start | bytes 995332
  63.0 17.9 %collective-permute-start.6 = (bf16[15,2,6,384]{3,2,1,0:T(8,128)(2,1)S(1)}, bf16[15,2,6,384]{3,2,1,0:T(8,128)(2,1)S(1)}, u32[]{:S(2)}, u32[]{:S(2)}) collective-permute-start(bf16[15,2,6,384]{3,2,1,0:T(8,128)(2,1)S(1)} %slice.59), channel_id=1, source_target_pairs={{0,16},{16,32},{32,48},{48,64},{64,80},{80,96},{96,112},{112,128},... | collective-permute-start | bytes 414728 | tf_op jit(solution)/shard_map/ppermute | solution.py:426
  64.7 16.2 %collective-permute-start.7 = (bf16[3,2,6,384]{3,2,1,0:T(8,128)(2,1)S(1)}, bf16[3,2,6,384]{3,2,1,0:T(8,128)(2,1)S(1)}, u32[]{:S(2)}, u32[]{:S(2)}) collective-permute-start(bf16[3,2,6,384]{3,2,1,0:T(8,128)(2,1)S(1)} %get-tuple-element.85), channel_id=1, source_target_pairs={{0,17},{1,18},{2,19},{3,20},{4,21},{5,22},{6,23},{7,24},{8,25},{9,... | collective-permute-start | bytes 82952 | tf_op jit(solution)/shard_map/ppermute | solution.py:434
  64.8 16.1 %collective-permute-start.5 = (bf16[3,2,6,384]{3,2,1,0:T(8,128)(2,1)S(1)}, bf16[3,2,6,384]{3,2,1,0:T(8,128)(2,1)S(1)}, u32[]{:S(2)}, u32[]{:S(2)}) collective-permute-start(bf16[3,2,6,384]{3,2,1,0:T(8,128)(2,1)S(1)} %get-tuple-element.86), channel_id=1, source_target_pairs={{0,1},{1,2},{2,3},{3,4},{4,5},{5,6},{6,7},{7,8},{8,9},{9,10},{10,1... | collective-permute-start | bytes 82952 | tf_op jit(solution)/shard_map/ppermute | solution.py:428
  76.2 14.8 %all-to-all-start.3 = ((bf16[16,32,96]{2,1,0:T(8,128)(2,1)}), bf16[16,32,96]{2,1,0:T(8,128)(2,1)S(1)}, u32[]{:S(2)}, u32[]{:S(2)}) async-start(bf16[16,32,96]{2,1,0:T(8,128)(2,1)} %get-tuple-element.54), calls=%async_computation.3 | async-start | bytes 262144 | tf_op jit(solution)/shard_map/all_to_all | solution.py:438

commit v4 on v3

--- a/solution.py
+++ b/solution.py
@@ -144,7 +144,7 @@
 def block_kernel(
     me_ref, x_ref, c_ref, gain_ref, w_same_ref, w_other_ref, bias_ref, order_ref,
     same_ref, other_ref, dq_s, dk_s, dv_s,
-    w_s, gw_s, normed_s, q_s, d_s, k_s, v_s, ctx_s, dsum_s, fold_s, pick_s, lines_s,
+    w_s, gw_s, normed_s, q_s, d_s, k_s, v_s, ctx_s, dsum_s, fold_s, pick_s, lines_s, bias_s, bias_sem,
     *, heads, windows, levels, lat_rows, rels,
 ):
     feat = x_ref.shape[1]
@@ -160,6 +160,8 @@
     part = packed // 4
     parity = me_ref[0] % 2
 
+    bias_copy = pltpu.make_async_copy(bias_ref, bias_s, bias_sem)
+    bias_copy.start()
     load_weights(w_s, w_same_ref, w_other_ref, parity)
     std, _ = normalise(x_ref)
     normed_s[...] = (std * gain_ref[...]).astype(BF16)
@@ -193,7 +195,7 @@
 
     def head(h, carry):
         qh, dh, kh, vh = q_s[h], d_s[h], k_s[h], v_s[h]
-        score = mm(kh, qh, TN) * (scale * LOG2E) + jnp.concatenate([bias_ref[h]] * windows, axis=1)
+        score = mm(kh, qh, TN) * (scale * LOG2E) + jnp.concatenate([bias_s[h]] * windows, axis=1)
         d_prob = mm(vh, dh, TN)
         expo = jnp.exp2(score - jnp.max(score, axis=0, keepdims=True))
         prob = expo * (1.0 / jnp.sum(expo, axis=0, keepdims=True))
@@ -219,6 +221,7 @@
             fold_s[g, pl.ds(h, cell, stride=slots), :] = folded[:, g * 128:(g + 1) * 128]
         return carry
 
+    bias_copy.wait()
     lax.fori_loop(0, heads, head, 0, unroll=True)
 
     def by_window(ref, w):
@@ -292,7 +295,7 @@
     return pl.pallas_call(
         functools.partial(block_kernel, heads=heads, windows=windows, levels=levels, lat_rows=lat_rows, rels=rels),
         out_shape=(sent, sent, jax.ShapeDtypeStruct((heads, dim, rows), BF16), aligned, aligned),
-        in_specs=[pl.BlockSpec(memory_space=pltpu.SMEM)] + [vmem] * 7,
+        in_specs=[pl.BlockSpec(memory_space=pltpu.SMEM)] + [vmem] * 5 + [pl.BlockSpec(memory_space=pl.ANY), vmem],
         out_specs=[vmem] * 5,
         scratch_shapes=[
             pltpu.VMEM((4, feat, feat), F32),
@@ -307,6 +310,8 @@
             pltpu.VMEM((tiles, (cell + 1) * slots, 128), F32),
             pltpu.VMEM((tokens, rows), BF16),
             pltpu.VMEM((2 * pairs, slots, feat), BF16),
+            pltpu.VMEM((heads, tokens, tokens), F32),
+            pltpu.SemaphoreType.DMA,
         ],
         compiler_params=pltpu.CompilerParams(vmem_limit_bytes=BLOCK_MB * 2**20),
         name="window_block",
@@ -489,11 +494,11 @@
     )
 
     paired = (g_same.astype(F32) + swap(g_other, "lon", 1).astype(F32)).astype(BF16)
-    paired, dq, dk, dv = lax.optimization_barrier((paired, dq, dk, dv))
+    d_input = input_gradient(me, shifted, gain, w_same, w_other, dq, dk, dv)
+    paired, d_input = lax.optimization_barrier((paired, d_input))
     arrived = spread_over_lon(paired)
     message, lines = sum_and_turn(arrived, lats, 4 * part)
     grad_query, grad_key, grad_value, grad_out, grad_gain = last_sum(spread_over_lat(message), part, feat)
-    d_input = input_gradient(me, shifted, gain, w_same, w_other, dq, dk, dv)
 
     d_in = d_input.reshape(lon_cols, levels, lat_rows, feat)
     stay = lon_cols - half_cols

time: 92.3 us -> 91.9 us (level)
  waiting for transfers between devices: 26 us -> 27.1 us
  local copies, waits for them, and re-layouts: 6.99 us -> 5.93 us
    all_to_all x2, waiting for transfers between devices: 8.94 us -> 11.2 us  [spread_over_lon(): return lax.all_to_all(x, 'lon', 0, 0, axis_index_groups=groups)]
    ppermute x2, waiting for transfers between devices: 1.93 us -> 0.74 us  [swap(): return lax.ppermute(x, axis, [(i, i ^ bit) for i in range(n)])]
    unnamed x15 -> x11, local copies, waits for them, and re-layouts: 4.95 us -> 3.89 us
where the time goes in v4:
time: 91.9 us; the launch traced here: 91.4 us
  starting transfers between devices  34.5 us (38%)
  waiting for transfers between devices  27.1 us (29%)
  Pallas kernels  17.9 us (19%)
  local copies, waits for them, and re-layouts  5.93 us (6%)
  other arithmetic  5.1 us (6%)
    all_to_all x2, starting transfers between devices, spread_over_lat(): return lax.all_to_all(x, 'lat', 0, 0)  15.7 us
    all_to_all x2, waiting for transfers between devices, spread_over_lat(): return lax.all_to_all(x, 'lat', 0, 0)  15.1 us
    all_to_all x2, starting transfers between devices, spread_over_lon(): return lax.all_to_all(x, 'lon', 0, 0, axis_index_groups=groups)  11.7 us
    all_to_all x2, waiting for transfers between devices, spread_over_lon(): return lax.all_to_all(x, 'lon', 0, 0, axis_index_groups=groups)  11.2 us
    pallas_call x1, Pallas kernels, run_block(): pl.pallas_call(functools.partial(block_kernel, heads=heads, windows=windo...  10.3 us
    pallas_call x1, Pallas kernels, make_bias(): pl.pallas_call(functools.partial(bias_kernel, levels=levels, lat_rows=lat...  3.99 us
    unnamed x11, local copies, waits for them, and re-layouts  3.89 us
    ppermute x2, starting transfers between devices, shift(): lax.ppermute(x, 'lat', [(i, (i + lat_by) % lats) for i in range(lats)])  3.84 us
  transfers between devices with their start and end apart: 12, of which 4 were waited for; matrix products, arithmetic and copies ran while one was open for 8% of the time, Pallas kernels for 7%

profile of v4, /device:TPU:8, one launch (start us, length us, event | category | flops | bytes accessed | tf_op | source)
XLA Modules:
  0.0 91.4 jit_solution(7856624249337428878)
XLA Ops:
  0.6 0.8 pad_maximum_fusion
  1.5 0.7 broadcast_in_dim.12
  2.1 11.0 %all-to-all-start = ((bf16[16,24,96]{2,1,0:T(8,128)(2,1)}), bf16[16,24,96]{2,1,0:T(8,128)(2,1)S(1)}, u32[]{:S(2)}, u32[]{:S(2)}) async-start(bf16[16,24,96]{2,1,0:T(8,128)(2,1)} %broadcast_in_dim.12), calls=%async_computation | async-start | bytes 196608 | tf_op jit(solution)/shard_map/all_to_all | solution.py:443
  13.2 1.0 %copy.32 = f32[1,12,6336]{2,1,0:T(8,128)S(1)} copy(f32[1,12,6336]{2,0,1:T(1,128)} %param.16) | data formatting | bytes 608256
  14.2 2.1 %maximum_bitcast_fusion = bf16[18,2,2,12,384]{4,2,0,3,1:T(2,128)(2,1)S(1)} fusion(bf16[1,2,12,18,384]{4,1,3,2,0:T(2,128)(2,1)} %bitcast.26, bf16[1,2,12,18,384]{4,1,3,2,0:T(2,128)(2,1)} %bitcast.27), kind=kLoop, calls=%fused_computation.3 | loop fusion | flops 331776 | bytes 1327104 | tf_op jit(solution)/shard_map/transpose | solution.py:466
  16.2 7.0 %all-to-all-done.x_ref = bf16[16,24,96]{2,1,0:T(8,128)(2,1)S(1)} async-done(((bf16[16,24,96]{2,1,0:T(8,128)(2,1)}), bf16[16,24,96]{2,1,0:T(8,128)(2,1)S(1)}, u32[]{:S(2)}, u32[]{:S(2)}) %all-to-all-start) | async-done | bytes 73760 | tf_op jit(solution)/shard_map/all_to_all | solution.py:443
  23.2 0.9 %turn_weights.1 = bf16[8,96,384]{2,1,0:T(8,128)(2,1)} custom-call(bf16[16,24,96]{2,1,0:T(8,128)(2,1)S(1)} %all-to-all-done.x_ref), custom_call_target="tpu_custom_call" | custom-call | tf_op jit(solution)/shard_map/turn_weights/pallas_call | solution.py:114
  24.2 5.1 %all-to-all-start.1 = ((bf16[8,96,384]{2,1,0:T(8,128)(2,1)}), bf16[8,96,384]{2,1,0:T(8,128)(2,1)S(1)}, u32[]{:S(2)}, u32[]{:S(2)}) async-start(bf16[8,96,384]{2,1,0:T(8,128)(2,1)} %turn_weights.1), calls=%async_computation.1 | async-start | bytes 1179648 | tf_op jit(solution)/shard_map/all_to_all | solution.py:449
  29.2 0.4 fusion.3
  29.6 2.2 %collective-permute-start = (bf16[15,2,2,6,384]{4,2,0,3,1:T(2,128)(2,1)S(1)}, bf16[15,2,2,6,384]{4,2,0,3,1:T(2,128)(2,1)S(1)}, u32[]{:S(2)}, u32[]{:S(2)}) collective-permute-start(bf16[15,2,2,6,384]{4,2,0,3,1:T(2,128)(2,1)S(1)} %get-tuple-element.79), channel_id=1, source_target_pairs={{0,240},{16,0},{32,16},{48,32},{64,48},{80,64},{96,80},{112,96},{1... | collective-permute-start | bytes 829448 | tf_op jit(solution)/shard_map/ppermute | solution.py:431
  32.0 0.3 collective-permute-start.1
  32.3 4.0 %make_bias.1.bias_ref = f32[12,144,144]{2,1,0:T(8,128)S(1)} custom-call(s32[1]{0:T(128)} %bitcast.1.last_ref, f32[12,6336]{1,0:T(8,128)S(1)} %bitcast.24, bf16[512,384]{1,0:T(8,128)(2,1)S(1)} %copy-done.1), custom_call_target="tpu_custom_call" | custom-call | tf_op jit(solution)/shard_map/make_bias/pallas_call | solution.py:89
  36.3 1.3 %copy-done = f32[12,144,144]{2,1,0:T(8,128)} copy-done((f32[12,144,144]{2,1,0:T(8,128)}, f32[12,144,144]{2,1,0:T(8,128)S(1)}, u32[]{:S(2)}) %copy-start) | copy-done | bytes 995352
  37.6 0.8 collective-permute-start.3
  38.4 1.0 %maximum_maximum_fusion = bf16[18,2,2,12,384]{4,2,0,3,1:T(2,128)(2,1)S(1)} fusion(bf16[3,2,2,6,384]{4,2,0,3,1:T(2,128)(2,1)S(1)} %collective-permute-done.2, bf16[3,2,2,6,384]{4,2,0,3,1:T(2,128)(2,1)S(1)} %collective-permute-done.1, bf16[15,2,2,6,384]{4,2,0,3,1:T(2,128)(2,1)S(1)} %collective-permute-done, bf16[15,2,2,6,384]{4,2,0,3,1:T(2,128)(2,1)S(1)} %get-tuple-element.36), kind=kLoop, calls=%fused_computation.4 | loop fusion | flops 995328 | bytes 1327104 | tf_op jit(solution)/shard_map/concatenate | solution.py:484
  39.4 0.5 fusion.1
  40.2 10.3 %window_block.1 = (bf16[8,112,384]{2,1,0:T(8,128)(2,1)S(1)}, bf16[8,112,384]{2,1,0:T(8,128)(2,1)S(1)}, bf16[12,32,432]{2,1,0:T(8,128)(2,1)S(1)}, bf16[12,96,144]...) custom-call(s32[1]{0:T(128)} %bitcast.me_ref, bf16[432,384]{1,0:T(8,128)(2,1)S(1)} %reshape_squeeze.6.x_ref, ...), custom_call_target="tpu_custom_call" | custom-call | tf_op jit(solution)/shard_map/window_block/pallas_call | solution.py:295
  50.5 0.3 collective-permute-start.4
  50.8 1.2 %input_gradient.1 = bf16[432,384]{1,0:T(8,128)(2,1)S(1)} custom-call(s32[1]{0:T(128)} %bitcast.me_ref, bf16[432,384]{1,0:T(8,128)(2,1)S(1)} %reshape_squeeze.6.x_ref, f32[1,384]{1,0:T(1,128)S(1)} %broadcast_in_dim.13.gain_ref, bf16[8,96,384]{2,1,0:T(8,128)(2,1)S(1)} %all-to-all-done.1.w_same_ref, bf16[8,96,384]{2,1,0:T(8,128)(2,1)S(1)} %collective-permute-done.3.w_other_ref, ...), custom_call_target="tpu_custom_call" | custom-call | tf_op jit(solution)/shard_map/input_gradient/pallas_call | solution.py:346
  52.0 0.7 collective-permute-done.4
  52.7 1.0 %add_convert_fusion = bf16[8,112,384]{2,1,0:T(8,128)(2,1)} fusion(bf16[8,112,384]{2,1,0:T(8,128)(2,1)S(1)} %collective-permute-done.4, bf16[8,112,384]{2,1,0:T(8,128)(2,1)S(1)} %get-tuple-element.42), kind=kLoop, calls=%fused_computation | loop fusion | flops 1376256 | bytes 2064384 | tf_op jit(solution)/shard_map/convert_element_type | solution.py:496
  53.7 6.6 %all-to-all-start.2 = ((bf16[8,112,384]{2,1,0:T(8,128)(2,1)}), bf16[8,112,384]{2,1,0:T(8,128)(2,1)S(1)}, u32[]{:S(2)}, u32[]{:S(2)}) async-start(bf16[8,112,384]{2,1,0:T(8,128)(2,1)} %add_convert_fusion), calls=%async_computation.2 | async-start | bytes 1376256 | tf_op jit(solution)/shard_map/all_to_all | solution.py:449
  60.5 1.7 %collective-permute-start.6 = (bf16[15,2,6,384]{3,2,1,0:T(8,128)(2,1)S(1)}, bf16[15,2,6,384]{3,2,1,0:T(8,128)(2,1)S(1)}, u32[]{:S(2)}, u32[]{:S(2)}) collective-permute-start(bf16[15,2,6,384]{3,2,1,0:T(8,128)(2,1)S(1)} %slice.59), channel_id=1, source_target_pairs={{0,16},{16,32},{32,48},{48,64},{64,80},{80,96},{96,112},{112,128},... | collective-permute-start | bytes 414728 | tf_op jit(solution)/shard_map/ppermute | solution.py:431
  62.3 1.6 %collective-permute-start.5 = (bf16[3,2,6,384]{3,2,1,0:T(8,128)(2,1)S(1)}, bf16[3,2,6,384]{3,2,1,0:T(8,128)(2,1)S(1)}, u32[]{:S(2)}, u32[]{:S(2)}) collective-permute-start(bf16[3,2,6,384]{3,2,1,0:T(8,128)(2,1)S(1)} %get-tuple-element.82), channel_id=1, source_target_pairs={{0,1},{1,2},{2,3},{3,4},{4,5},{5,6},{6,7},{7,8},{8,9},{9,10},{10,1... | collective-permute-start | bytes 82952 | tf_op jit(solution)/shard_map/ppermute | solution.py:433
  63.9 11.2 %all-to-all-done.2.x_ref = bf16[8,112,384]{2,1,0:T(8,128)(2,1)S(1)} async-done(((bf16[8,112,384]{2,1,0:T(8,128)(2,1)}), bf16[8,112,384]{2,1,0:T(8,128)(2,1)S(1)}, u32[]{:S(2)}, u32[]{:S(2)}) %all-to-all-start.2) | async-done | bytes 688160 | tf_op jit(solution)/shard_map/all_to_all | solution.py:449
  75.1 0.9 sum_and_turn.1
  75.9 4.7 %all-to-all-start.3 = ((bf16[16,32,96]{2,1,0:T(8,128)(2,1)}), bf16[16,32,96]{2,1,0:T(8,128)(2,1)S(1)}, u32[]{:S(2)}, u32[]{:S(2)}) async-start(bf16[16,32,96]{2,1,0:T(8,128)(2,1)} %get-tuple-element.50), calls=%async_computation.3 | async-start | bytes 262144 | tf_op jit(solution)/shard_map/all_to_all | solution.py:443
  80.7 0.6 copy.28
  81.4 0.2 fusion
  81.6 1.0 %copy.27 = bf16[2,12,18,384]{3,0,2,1:T(2,128)(2,1)} copy(bf16[2,12,18,384]{3,1,0,2:T(8,128)(2,1)S(1)} %fusion) | data formatting | bytes 663552
  82.6 8.1 %all-to-all-done.3.x_ref = bf16[16,32,96]{2,1,0:T(8,128)(2,1)S(1)} async-done(((bf16[16,32,96]{2,1,0:T(8,128)(2,1)}), bf16[16,32,96]{2,1,0:T(8,128)(2,1)S(1)}, u32[]{:S(2)}, u32[]{:S(2)}) %all-to-all-start.3) | async-done | bytes 98336 | tf_op jit(solution)/shard_map/all_to_all | solution.py:443
  90.7 0.7 last_sum.1
  (31 shorter events, 0.8 us)
Async XLA Ops:
  2.1 21.1 %all-to-all-start = ((bf16[16,24,96]{2,1,0:T(8,128)(2,1)}), bf16[16,24,96]{2,1,0:T(8,128)(2,1)S(1)}, u32[]{:S(2)}, u32[]{:S(2)}) async-start(bf16[16,24,96]{2,1,0:T(8,128)(2,1)} %broadcast_in_dim.12), calls=%async_computation | async-start | bytes 196608 | tf_op jit(solution)/shard_map/all_to_all | solution.py:443
  24.2 8.1 %copy-start.1 = (bf16[512,384]{1,0:T(8,128)(2,1)S(1)}, bf16[512,384]{1,0:T(8,128)(2,1)}, u32[]{:S(2)}) copy-start(bf16[512,384]{1,0:T(8,128)(2,1)} %constant.11.clone.order_ref) | copy-start | bytes 1179652
  24.2 13.4 %all-to-all-start.1 = ((bf16[8,96,384]{2,1,0:T(8,128)(2,1)}), bf16[8,96,384]{2,1,0:T(8,128)(2,1)S(1)}, u32[]{:S(2)}, u32[]{:S(2)}) async-start(bf16[8,96,384]{2,1,0:T(8,128)(2,1)} %turn_weights.1), calls=%async_computation.1 | async-start | bytes 1179648 | tf_op jit(solution)/shard_map/all_to_all | solution.py:449
  29.6 8.8 %copy-start.3 = (f32[384]{0:T(512)S(1)}, f32[384]{0:T(512)}, u32[]{:S(2)}) copy-start(f32[384]{0:T(512)} %param.11) | copy-start | bytes 4612
  29.6 7.9 %collective-permute-start = (bf16[15,2,2,6,384]{4,2,0,3,1:T(2,128)(2,1)S(1)}, bf16[15,2,2,6,384]{4,2,0,3,1:T(2,128)(2,1)S(1)}, u32[]{:S(2)}, u32[]{:S(2)}) collective-permute-start(bf16[15,2,2,6,384]{4,2,0,3,1:T(2,128)(2,1)S(1)} %get-tuple-element.79), channel_id=1, source_target_pairs={{0,240},{16,0},{32,16},{48,32},{64,48},{80,64},{96,80},{112,96},{1... | collective-permute-start | bytes 829448 | tf_op jit(solution)/shard_map/ppermute | solution.py:431
  31.9 5.7 %collective-permute-start.2 = (bf16[3,2,2,6,384]{4,2,0,3,1:T(2,128)(2,1)S(1)}, bf16[3,2,2,6,384]{4,2,0,3,1:T(2,128)(2,1)S(1)}, u32[]{:S(2)}, u32[]{:S(2)}) collective-permute-start(bf16[3,2,2,6,384]{4,2,0,3,1:T(2,128)(2,1)S(1)} %get-tuple-element.77), channel_id=1, source_target_pairs={{0,255},{1,240},{2,241},{3,242},{4,243},{5,244},{6,245},{7,246},{8... | collective-permute-start | bytes 165896 | tf_op jit(solution)/shard_map/ppermute | solution.py:439
  32.0 5.6 %collective-permute-start.1 = (bf16[3,2,2,6,384]{4,2,0,3,1:T(2,128)(2,1)S(1)}, bf16[3,2,2,6,384]{4,2,0,3,1:T(2,128)(2,1)S(1)}, u32[]{:S(2)}, u32[]{:S(2)}) collective-permute-start(bf16[3,2,2,6,384]{4,2,0,3,1:T(2,128)(2,1)S(1)} %get-tuple-element.78), channel_id=1, source_target_pairs={{0,15},{1,0},{2,1},{3,2},{4,3},{5,4},{6,5},{7,6},{8,7},{9,8},{10,9... | collective-permute-start | bytes 165896 | tf_op jit(solution)/shard_map/ppermute | solution.py:433
  36.3 1.3 %copy-start = (f32[12,144,144]{2,1,0:T(8,128)}, f32[12,144,144]{2,1,0:T(8,128)S(1)}, u32[]{:S(2)}) copy-start(f32[12,144,144]{2,1,0:T(8,128)S(1)} %make_bias.1.bias_ref) | copy-start | bytes 2985988
  37.6 2.6 %collective-permute-start.3 = (bf16[8,96,384]{2,1,0:T(8,128)(2,1)S(1)}, bf16[8,96,384]{2,1,0:T(8,128)(2,1)S(1)}, u32[]{:S(2)}, u32[]{:S(2)}) collective-permute-start(bf16[8,96,384]{2,1,0:T(8,128)(2,1)S(1)} %all-to-all-done.1.w_same_ref), channel_id=1, source_target_pairs={{0,1},{1,0},{2,3},{3,2},{4,5},{5,4},{6,7},{7,6},{8,9},{9,8},{10,11... | collective-permute-start | bytes 1769480 | tf_op jit(solution)/shard_map/ppermute | solution.py:425
  50.5 2.2 %collective-permute-start.4 = (bf16[8,112,384]{2,1,0:T(8,128)(2,1)S(1)}, bf16[8,112,384]{2,1,0:T(8,128)(2,1)S(1)}, u32[]{:S(2)}, u32[]{:S(2)}) collective-permute-start(bf16[8,112,384]{2,1,0:T(8,128)(2,1)S(1)} %get-tuple-element.43), channel_id=1, source_target_pairs={{0,1},{1,0},{2,3},{3,2},{4,5},{5,4},{6,7},{7,6},{8,9},{9,8},{10,11... | collective-permute-start | bytes 2064392 | tf_op jit(solution)/shard_map/ppermute | solution.py:425
  53.7 21.3 %all-to-all-start.2 = ((bf16[8,112,384]{2,1,0:T(8,128)(2,1)}), bf16[8,112,384]{2,1,0:T(8,128)(2,1)S(1)}, u32[]{:S(2)}, u32[]{:S(2)}) async-start(bf16[8,112,384]{2,1,0:T(8,128)(2,1)} %add_convert_fusion), calls=%async_computation.2 | async-start | bytes 1376256 | tf_op jit(solution)/shard_map/all_to_all | solution.py:449
  60.3 21.0 %copy-start.2 = (bf16[2,12,18,384]{3,0,2,1:T(2,128)(2,1)S(1)}, bf16[2,12,18,384]{3,0,2,1:T(2,128)(2,1)}, u32[]{:S(2)}) copy-start(bf16[2,12,18,384]{3,0,2,1:T(2,128)(2,1)} %param.10) | copy-start | bytes 995332
  60.5 20.2 %collective-permute-start.6 = (bf16[15,2,6,384]{3,2,1,0:T(8,128)(2,1)S(1)}, bf16[15,2,6,384]{3,2,1,0:T(8,128)(2,1)S(1)}, u32[]{:S(2)}, u32[]{:S(2)}) collective-permute-start(bf16[15,2,6,384]{3,2,1,0:T(8,128)(2,1)S(1)} %slice.59), channel_id=1, source_target_pairs={{0,16},{16,32},{32,48},{48,64},{64,80},{80,96},{96,112},{112,128},... | collective-permute-start | bytes 414728 | tf_op jit(solution)/shard_map/ppermute | solution.py:431
  62.2 18.4 %collective-permute-start.7 = (bf16[3,2,6,384]{3,2,1,0:T(8,128)(2,1)S(1)}, bf16[3,2,6,384]{3,2,1,0:T(8,128)(2,1)S(1)}, u32[]{:S(2)}, u32[]{:S(2)}) collective-permute-start(bf16[3,2,6,384]{3,2,1,0:T(8,128)(2,1)S(1)} %get-tuple-element.81), channel_id=1, source_target_pairs={{0,17},{1,18},{2,19},{3,20},{4,21},{5,22},{6,23},{7,24},{8,25},{9,... | collective-permute-start | bytes 82952 | tf_op jit(solution)/shard_map/ppermute | solution.py:439
  62.3 18.4 %collective-permute-start.5 = (bf16[3,2,6,384]{3,2,1,0:T(8,128)(2,1)S(1)}, bf16[3,2,6,384]{3,2,1,0:T(8,128)(2,1)S(1)}, u32[]{:S(2)}, u32[]{:S(2)}) collective-permute-start(bf16[3,2,6,384]{3,2,1,0:T(8,128)(2,1)S(1)} %get-tuple-element.82), channel_id=1, source_target_pairs={{0,1},{1,2},{2,3},{3,4},{4,5},{5,6},{6,7},{7,8},{8,9},{9,10},{10,1... | collective-permute-start | bytes 82952 | tf_op jit(solution)/shard_map/ppermute | solution.py:433
  75.9 14.8 %all-to-all-start.3 = ((bf16[16,32,96]{2,1,0:T(8,128)(2,1)}), bf16[16,32,96]{2,1,0:T(8,128)(2,1)S(1)}, u32[]{:S(2)}, u32[]{:S(2)}) async-start(bf16[16,32,96]{2,1,0:T(8,128)(2,1)} %get-tuple-element.50), calls=%async_computation.3 | async-start | bytes 262144 | tf_op jit(solution)/shard_map/all_to_all | solution.py:443
